TPU v7x, 128 devices: a whole 4x4x4 slice. The times are simulated.
128 devices in a mesh: grp: 4 (over z), dom: 32 (over y, x, core).
Axes of the slice: x: 4, y: 4, z: 4, core: 2. Of those that a mesh axis runs over, the one named last changes fastest.
Arguments:
- features: bfloat16 [32768, 768], P(('grp', 'dom')), may hold values from -6 to 6
- text_embed: bfloat16 [32768, 512], P(('grp', 'dom')), may hold values from -6 to 6
- adjacency: bfloat16 [32768, 1024], P(('grp', 'dom')), may hold values from 0 to 0.0625
- block_cols: int32 [256, 8], P(('grp', 'dom')), may hold values from 0 to 255
- positive: int32 [32768], P(('grp', 'dom')), may hold values from 0 to 32767
- self_weight: bfloat16 [768, 512], replicated, may hold values from -0.21875 to 0.21875
- nbr_weight: bfloat16 [768, 512], replicated, may hold values from -0.21875 to 0.21875
- hidden_bias: float32 [512], replicated, may hold values from -3 to 3
Outputs:
- embedding: bfloat16 [32768, 512], P(('grp', 'dom'))
- mean_loss: float32 [], replicated
- grad_self: float32 [768, 512], replicated
- grad_nbr: float32 [768, 512], replicated
- grad_bias: float32 [512], replicated
All inputs are finite; a program needn't handle non-finite values.
Results may differ from a plain program's by a relative error of at most 0.0118.
Values may be sent and summed in bfloat16 or wider, within the bound.
A program may use at most 192 MiB of HBM per device.

v0:
```python
import jax
import jax.numpy as jnp
from jax import lax
from jax.sharding import PartitionSpec as P

BLOCK = 128


epsilon = 1e-05
inverse_softmax_coldness = 10.0
highest = lax.Precision.HIGHEST


def rms_scale(values):
    return lax.rsqrt(jnp.mean(values * values, axis=1, keepdims=True) + epsilon)


def shards(
    features, text_embed, adjacency, block_cols, positive, self_weight, nbr_weight, hidden_bias
):
    node_count = features.shape[0]
    width_in = features.shape[1]
    result_dimension = self_weight.shape[1]
    rows_per_block = BLOCK
    row_blocks = node_count // rows_per_block
    fan_blocks = block_cols.shape[1]
    dom_size = lax.axis_size("dom")
    grp_size = lax.axis_size("grp")
    my_group = lax.axis_index("grp")
    device_of = block_cols // row_blocks
    group_of = device_of // dom_size
    domain_of = device_of % dom_size
    within = block_cols % row_blocks
    same_group = group_of == my_group
    lookup_position = jnp.where(
        same_group,
        domain_of * row_blocks + within,
        dom_size * row_blocks + group_of * row_blocks + within,
    ).reshape(-1)
    adj_rows = adjacency.reshape(row_blocks, rows_per_block, fan_blocks * rows_per_block)
    self_term = jnp.dot(features, self_weight, preferred_element_type=jnp.float32)
    gathered_group = lax.all_gather(features, "dom", axis=0, tiled=True)
    gathered_cross = lax.all_gather(features, "grp", axis=0, tiled=True)
    panel_table = jnp.concatenate([gathered_group, gathered_cross], axis=0).reshape(
        -1, rows_per_block, width_in
    )
    chosen = panel_table[lookup_position].reshape(row_blocks, fan_blocks * rows_per_block, width_in)
    aggregated = jnp.einsum(
        "rbm,rmd->rbd", adj_rows, chosen, preferred_element_type=jnp.float32
    ).reshape(node_count, width_in)
    nbr_term = jnp.dot(aggregated, nbr_weight.astype(jnp.float32), precision=highest)
    pre_act = self_term + nbr_term + hidden_bias
    hidden = jnp.maximum(pre_act, 0.0)
    scale_rows = rms_scale(hidden)
    normed = hidden * scale_rows
    half_unit_vector = normed.astype(jnp.bfloat16)
    text_wide = text_embed.astype(jnp.float32)
    text_unit = (text_wide * rms_scale(text_wide)).astype(jnp.bfloat16)
    normalizing_multiplier = inverse_softmax_coldness / result_dimension
    block_text = lax.all_gather(text_unit, ("grp", "dom"), axis=0, tiled=True)
    similarity_logits = (
        jnp.dot(half_unit_vector, block_text.T, preferred_element_type=jnp.float32)
        * normalizing_multiplier
    )
    exponent = jnp.exp(similarity_logits)
    columns = jnp.arange(block_text.shape[0], dtype=jnp.int32)
    onehot = (positive[:, None] == columns[None, :]).astype(jnp.bfloat16)
    totals = jnp.sum(exponent, axis=1)
    weighted = jnp.dot(
        exponent.astype(jnp.bfloat16), block_text, preferred_element_type=jnp.float32
    )
    picked = jnp.dot(onehot, block_text, preferred_element_type=jnp.float32)
    totals, weighted, picked = (totals, weighted, picked)
    pos_logit = (
        jnp.sum(half_unit_vector.astype(jnp.float32) * picked, axis=1) * normalizing_multiplier
    )
    loss_part = jnp.sum(jnp.log(totals) - pos_logit)
    grad_unit = normalizing_multiplier * (weighted / totals[:, None] - picked)
    grad_hidden = scale_rows * (
        grad_unit - normed * jnp.mean(grad_unit * normed, axis=1, keepdims=True)
    )
    grad_pre = jnp.where(pre_act > 0, grad_hidden, 0.0)
    grad_self = jnp.dot(features.astype(jnp.float32).T, grad_pre, precision=highest)
    grad_nbr = jnp.dot(aggregated.T, grad_pre, precision=highest)
    grad_bias = jnp.sum(grad_pre, axis=0)
    summed = lax.psum((grad_self, grad_nbr, grad_bias, loss_part), ("grp", "dom"))
    mean_loss = summed[3] / (node_count * dom_size * grp_size)
    return (hidden.astype(jnp.bfloat16), mean_loss, summed[0], summed[1], summed[2])


def solution(mesh):
    in_specs = (
        P(("grp", "dom"), None),
        P(("grp", "dom"), None),
        P(("grp", "dom"), None),
        P(("grp", "dom"), None),
        P(("grp", "dom")),
        P(),
        P(),
        P(),
    )
    out_specs = (P(("grp", "dom"), None), P(), P(), P(), P())
    return jax.shard_map(shards, mesh=mesh, in_specs=in_specs, out_specs=out_specs, check_vma=False)
```

profile of v0, /device:TPU:1, one launch (start us, length us, event | category | flops | bytes accessed | tf_op | source)
XLA Modules:
  0.0 441.4 jit_solution(7458375105679085079)
XLA Ops:
  7.2 0.0 copy-start
  7.2 0.0 all-gather.6.cloned.1.call-start
  7.2 0.7 all-gather.6.cloned.1.call-update
  7.9 0.0 all-gather.4.cloned.1.call-start
  8.0 0.7 all-gather.4.cloned.1.call-update
  8.7 0.0 all-gather.8.cloned.1.call-start
  8.7 1.1 fusion.15
  9.8 1.8 fusion.16
  11.6 0.0 all-gather.8.cloned.1.call-update
  11.6 0.0 all-reduce.4.cloned.1.call-start
  11.6 0.7 compare_select_fusion.1
  12.4 0.1 reshape.77
  12.5 0.0 copy-start.4
  12.5 0.0 copy-start.3
  12.5 0.0 copy-start.2
  12.5 0.0 copy-start.5
  12.5 27.2 %all-gather.6.cloned.1.call-done = bf16[1024,768]{1,0:T(8,128)(2,1)} async-done(((bf16[256,768]{1,0:T(8,128)(2,1)}), bf16[1024,768]{1,0:T(8,128)(2,1)}) %all-gather.6.cloned.1.call-update) | async-done | bytes 1572880 | tf_op jit(solution)/shard_map/all_gather | solution.py:43
  39.7 65.4 %all-gather.4.cloned.1.call-done = bf16[8192,768]{1,0:T(8,128)(2,1)} async-done(((bf16[256,768]{1,0:T(8,128)(2,1)}), bf16[8192,768]{1,0:T(8,128)(2,1)}) %all-gather.4.cloned.1.call-update) | async-done | bytes 12582928 | tf_op jit(solution)/shard_map/all_gather | solution.py:42
  105.1 16.0 %pad_maximum_fusion = bf16[9216,768]{1,0:T(8,128)(2,1)} fusion(bf16[1024,768]{1,0:T(8,128)(2,1)} %all-gather.6.cloned.1.call-done, bf16[8192,768]{1,0:T(8,128)(2,1)} %all-gather.4.cloned.1.call-done), kind=kLoop, calls=%fused_computation.8 | loop fusion | flops 28311552 | bytes 28311552 | tf_op jit(solution)/shard_map/concatenate | solution.py:44
  121.1 0.0 copy-start.6
  121.1 7.5 %gather_fusion = bf16[16,128,768]{2,1,0:T(8,128)(2,1)} fusion(bf16[72,128,768]{2,1,0:T(8,128)(2,1)} %bitcast.24, s32[1024]{0:T(1024)S(1)} %pad_clamp_fusion), kind=kCustom, calls=%fused_computation | custom fusion | bytes 6291520 | tf_op jit(solution)/shard_map/gather | solution.py:47
  128.6 0.0 copy-done.4
  128.6 2.5 fusion.24
  131.1 0.0 copy-done.3
  131.1 0.8 fusion.22
  131.9 0.0 copy-done
  131.9 0.0 copy-done.2
  131.9 0.0 copy-done.5
  132.0 1.1 maximum_convert_fusion
  133.0 0.1 multiply_reduce_fusion.2
  133.2 81.8 %all-gather.8.cloned.1.call-done = bf16[32768,512]{1,0:T(8,128)(2,1)} async-done(((bf16[256,512]{1,0:T(8,128)(2,1)}), bf16[32768,512]{1,0:T(8,128)(2,1)}) %all-gather.8.cloned.1.call-update) | async-done | bytes 33554448 | tf_op jit(solution)/shard_map/all_gather | solution.py:60
  215.0 0.0 copy-done.6
  215.0 15.4 %fusion.1 = f32[256,512]{1,0:T(8,128)} fusion(bf16[32768,512]{1,0:T(8,128)(2,1)} %all-gather.8.cloned.1.call-done, s32[256]{0:T(256)S(1)} %copy-done.6), kind=kOutput, calls=%fused_computation.4 | convolution fusion | flops 8598323200 | bytes 34079744 | tf_op jit(solution)/shard_map/dot_general | solution.py:72
  230.4 0.0 copy-start.7
  230.4 19.2 %fusion.21 = (f32[256]{0:T(256)S(1)}, bf16[256,32768]{1,0:T(8,128)(2,1)}) fusion(bf16[32768,512]{1,0:T(8,128)(2,1)} %all-gather.8.cloned.1.call-done, f32[256,512]{1,0:T(8,128)S(1)} %get-tuple-element.19, f32[256]{0:T(256)S(1)} %add_rsqrt_fusion.1), kind=kOutput, calls=%fused_computation.46 | convolution fusion | flops 8615493632 | bytes 50857984 | tf_op jit(solution)/shard_map/dot_general | solution.py:62
  249.6 0.0 copy-done.7
  249.6 0.0 copy-start.1
  249.6 20.4 %multiply_reduce_fusion = (f32[256]{0:T(256)S(1)}, f32[256]{0:T(256)S(1)}, f32[256,512]{1,0:T(8,128)S(1)}) fusion(f32[256,512]{1,0:T(8,128)S(1)} %get-tuple-element.19, f32[256]{0:T(256)S(1)} %add_rsqrt_fusion.1, f32[256,512]{1,0:T(8,128)S(1)} %copy-done.7, f32[256]{0:T(256)S(1)} %get-tuple-element.20, bf16[32768,512]{1,0:T(8,128)(2,1)} %all-gather.8.cloned.1.call-done, ...), kind=kOutput, calls=%fused_computation.20 | convolution fusion | flops 8591376384 | bytes 51908608 | tf_op jit(solution)/shard_map/dot_general | solution.py:69
  270.0 0.6 subtract_reduce_fusion
  270.6 0.2 fusion.20
  270.9 2.6 fusion.23
  273.4 2.1 convolution_bitcast_fusion
  275.5 0.0 all-reduce.4.cloned.1.call-update
  275.5 64.8 %all-reduce = (f32[]{:T(128)}, f32[512]{0:T(512)}) all-reduce(f32[]{:T(128)} %get-tuple-element.23, f32[512]{0:T(512)S(1)} %get-tuple-element.16), channel_id=1, replica_groups=mesh['grp'=4,'dom'=32] {'grp','dom'}, use_global_device_ids=true, to_apply=%region_5.6 | all-reduce | flops 513 | bytes 4104 | tf_op jit(solution)/shard_map/psum | solution.py:86
  341.0 87.0 %all-reduce.4.cloned.1.call-done = (f32[768,512]{0,1:T(8,128)}, f32[768,512]{1,0:T(8,128)}) async-done(((f32[768,512]{0,1:T(8,128)}, f32[768,512]{1,0:T(8,128)}), (f32[768,512]{0,1:T(8,128)}, f32[768,512]{1,0:T(8,128)})) %all-reduce.4.cloned.1.call-update) | async-done | bytes 3145744 | tf_op jit(solution)/shard_map/psum | solution.py:86
  428.0 3.0 copy.13
  431.0 2.7 copy.16
  433.7 0.0 copy-done.1
  (4 shorter events, 0.0 us)
Async XLA Ops:
  7.2 124.8 %copy-start = (bf16[768,512]{1,0:T(8,128)(2,1)S(1)}, bf16[768,512]{1,0:T(8,128)(2,1)}, u32[]{:S(2)}) copy-start(bf16[768,512]{1,0:T(8,128)(2,1)} %param.13) | copy-start | bytes 2359300
  7.2 32.5 %all-gather.6.cloned.1.call-start = ((), (), s32[]{:S(2)}) async-start(), calls=%async_computation.1 | async-start | bytes 1966080 | tf_op jit(solution)/shard_map/all_gather | solution.py:43
  7.9 97.1 %all-gather.4.cloned.1.call-start = ((), (), s32[]{:S(2)}) async-start(), calls=%async_computation | async-start | bytes 12976128 | tf_op jit(solution)/shard_map/all_gather | solution.py:42
  8.7 206.3 %all-gather.8.cloned.1.call-start = ((), (), s32[]{:S(2)}) async-start(), calls=%async_computation.2 | async-start | bytes 33816576 | tf_op jit(solution)/shard_map/all_gather | solution.py:60
  11.6 416.4 %all-reduce.4.cloned.1.call-start = ((), (), s32[]{:S(2)}) async-start(), calls=%async_computation.3 | async-start | bytes 6291456 | tf_op jit(solution)/shard_map/psum | solution.py:86
  12.5 116.2 %copy-start.4 = (bf16[256,1024]{1,0:T(8,128)(2,1)S(1)}, bf16[256,1024]{1,0:T(8,128)(2,1)}, u32[]{:S(2)}) copy-start(bf16[256,1024]{1,0:T(8,128)(2,1)} %param.10) | copy-start | bytes 1572868
  12.5 118.7 %copy-start.3 = (bf16[768,512]{1,0:T(8,128)(2,1)S(1)}, bf16[768,512]{1,0:T(8,128)(2,1)}, u32[]{:S(2)}) copy-start(bf16[768,512]{1,0:T(8,128)(2,1)} %param.14) | copy-start | bytes 2359300
  12.5 119.5 %copy-start.2 = (bf16[256,768]{1,0:T(8,128)(2,1)S(1)}, bf16[256,768]{1,0:T(8,128)(2,1)}, u32[]{:S(2)}) copy-start(bf16[256,768]{1,0:T(8,128)(2,1)} %param.8) | copy-start | bytes 1179652
  12.5 119.5 %copy-start.5 = (f32[512]{0:T(512)S(1)}, f32[512]{0:T(512)}, u32[]{:S(2)}) copy-start(f32[512]{0:T(512)} %param.15) | copy-start | bytes 6148
  121.1 93.9 %copy-start.6 = (s32[256]{0:T(256)S(1)}, s32[256]{0:T(256)}, u32[]{:S(2)}) copy-start(s32[256]{0:T(256)} %param.12) | copy-start | bytes 3076
  230.4 19.2 %copy-start.7 = (f32[256,512]{1,0:T(8,128)S(1)}, f32[256,512]{1,0:T(8,128)}, u32[]{:S(2)}) copy-start(f32[256,512]{1,0:T(8,128)} %fusion.1) | copy-start | bytes 1572868
  249.6 184.1 %copy-start.1 = (bf16[768,512]{1,0:T(8,128)(2,1)S(1)}, bf16[768,512]{1,0:T(8,128)(2,1)}, u32[]{:S(2)}) copy-start(bf16[768,512]{1,0:T(8,128)(2,1)} %param.13) | copy-start | bytes 2359300
Sparse Core Ops, SparseCore 0:
  9.7 29.9 all-gather.5
  41.9 63.0 all-gather.3
  108.6 106.3 all-gather.7
  275.6 152.3 all-reduce.3
where the time goes:
time: 442 us; the launch traced here: 441 us
  waiting for transfers between devices  263 us (60%)
  blocking collectives  64.8 us (15%)
  matrix products  64 us (14%)
  other arithmetic  20.5 us (5%)
  between operations  15.7 us (4%)
  local copies, waits for them, and re-layouts  13.4 us (3%)
    psum x1, waiting for transfers between devices, shards(): lax.psum((grad_self, grad_nbr, grad_bias, loss_part), ('grp', 'dom'))  87 us
    all_gather x1, waiting for transfers between devices, shards(): block_text = lax.all_gather(text_unit, ('grp', 'dom'), axis=0, tiled=True)  81.8 us
    all_gather x1, waiting for transfers between devices, shards(): gathered_group = lax.all_gather(features, 'dom', axis=0, tiled=True)  65.4 us
    psum x1, blocking collectives, shards(): lax.psum((grad_self, grad_nbr, grad_bias, loss_part), ('grp', 'dom'))  64.8 us
    all_gather x1, waiting for transfers between devices, shards(): gathered_cross = lax.all_gather(features, 'grp', axis=0, tiled=True)  27.2 us
    dot_general x1, matrix products, shards(): jnp.dot(exponent.astype(jnp.bfloat16), block_text, preferred_element_type...  20.4 us
    dot_general x1, matrix products, shards(): jnp.dot(half_unit_vector, block_text.T, preferred_element_type=jnp.float32)  19.2 us
    concatenate x1, other arithmetic, shards(): jnp.concatenate([gathered_group, gathered_cross], axis=0)  16 us
  transfers between devices with their start and end apart: 4, of which 4 were waited for; matrix products, arithmetic and copies ran while one was open for 7% of the time, Pallas kernels for 0%

commit v1 on v0

v1 whole, which is shorter than its diff:
```python
import functools

import jax
import jax.numpy as jnp
from jax import lax
from jax.experimental import pallas as pl
from jax.experimental.pallas import tpu as pltpu
from jax.sharding import PartitionSpec as P

MESH = pl.DeviceIdType.MESH
D = 768
H = 512
BLOCK = 128
K = 8
ROWS = 256
HALF = 128
N_GRP = 4
N_DOM = 32
NODES = 32768
SLAB = N_DOM * ROWS
CHUNK = 1024

EPS = 1e-05
SCALE = 10.0 / H
LOG2E = 1.4426950408889634

BF = jnp.bfloat16
F32 = jnp.float32

STEPS = (0, -1, 1, 2)
GATHER_SEMS = 36


def rms_scale(values):
    return lax.rsqrt(jnp.mean(values * values, axis=1, keepdims=True) + EPS)


def dot(a, b):
    return jnp.dot(a, b, preferred_element_type=F32)


def dot_nt(a, b):
    return lax.dot_general(a, b, (((1,), (1,)), ((), ())), preferred_element_type=F32)


def dot_tn(a, b):
    return lax.dot_general(a, b, (((0,), (0,)), ((), ())), preferred_element_type=F32)


def kernel(
    feat, text, adj, cols, pos, self_w, nbr_w, bias,
    emb, grads, extra_out,
    F, T, Q, POS, AGG, HID, G, WACC, TACC, WP_S, WP_R, TOT_S, TOT_R,
    SA, RA, SB, RB, SC, RC, EX,
    fs, fr, ts, tr, zs, zr, ms, mr, gs, gr,
):
    g = lax.axis_index("grp")
    d = lax.axis_index("dom")
    c = d % 2
    x = (d // 2) % 4
    y = d // 8

    def dom_at(i, j, cc):
        ux, uy = 1 - cc, cc
        ax = (x + i * ux + j * uy + 4) % 4
        ay = (y + i * uy + j * ux + 4) % 4
        return (ay * 4 + ax) * 2 + cc

    def prim(k):
        return (g, dom_at(k, 0, c))

    def sec(k):
        return (g, dom_at(0, k, c))

    def zed(k):
        return ((g + k) % 4, d)

    sib = (g, d + 1 - 2 * c)
    pi = x * (1 - c) + y * c
    si = x * c + y * (1 - c)

    def rcopy(src, dst, ssem, rsem, dev):
        return pltpu.make_async_remote_copy(
            src_ref=src, dst_ref=dst, send_sem=ssem, recv_sem=rsem,
            device_id=dev, device_id_type=MESH,
        )

    pending = []

    def send(src, dst, ssem, rsem, dev):
        cp = rcopy(src, dst, ssem, rsem, dev)
        cp.start()
        pending.append(cp)

    def landed(region, ssem, rsem):
        rcopy(region, region, ssem, rsem, sib).wait_recv()

    barrier = pltpu.get_barrier_semaphore()
    partners = [sib] + [f(k) for f in (prim, sec, zed) for k in (1, 2, 3)]
    for dev in partners:
        pl.semaphore_signal(barrier, inc=1, device_id=dev, device_id_type=MESH)

    own = pl.ds(d * ROWS, ROWS)
    F[own, :] = feat[...]
    tw = text[...].astype(F32)
    T[own, :] = (tw * rms_scale(tw)).astype(BF)
    POS[g] = pos[...]
    pl.semaphore_wait(barrier, len(partners))

    class Gather:
        def __init__(self, tab, ssem, rsem):
            self.tab, self.ss, self.rs = tab, ssem, rsem

        def shard(self, i, j, cc, half=None):
            base = dom_at(i, j, cc) * ROWS
            if half is None:
                return self.tab.at[pl.ds(base, ROWS)]
            return self.tab.at[pl.ds(base + half * HALF, HALF)]

        def send(self, i, j, half, k, dev):
            ref = self.shard(i, j, c, half)
            send(ref, ref, self.ss.at[k], self.rs.at[k], dev)

        def wait(self, i, j, half, k, cc=None):
            ref = self.shard(i, j, c if cc is None else cc, half)
            landed(ref, self.ss.at[k], self.rs.at[k])

        def across(self, a, b):
            self.send(STEPS[a], STEPS[b], None, 20 + 4 * a + b, sib)

        def along(self, a):
            self.send(STEPS[a], 0, None, 4 + 4 * a, sec(1))
            self.send(STEPS[a], 0, None, 5 + 4 * a, sec(-1))

        def first(self):
            self.send(0, 0, None, 0, prim(1))
            self.send(0, 0, None, 1, prim(-1))
            self.along(0)
            self.across(0, 0)

        def second(self):
            self.wait(-1, 0, None, 0)
            self.send(-1, 0, 0, 2, prim(1))
            self.along(1)
            self.across(1, 0)
            self.wait(1, 0, None, 1)
            self.send(1, 0, 1, 3, prim(-1))
            self.along(2)
            self.across(2, 0)

        def turn(self, a):
            self.wait(STEPS[a], -1, None, 4 + 4 * a)
            self.send(STEPS[a], -1, 0, 6 + 4 * a, sec(1))
            self.across(a, 1)
            self.wait(STEPS[a], 1, None, 5 + 4 * a)
            self.send(STEPS[a], 1, 1, 7 + 4 * a, sec(-1))
            self.across(a, 2)

        def third(self):
            self.wait(2, 0, 0, 2)
            self.wait(2, 0, 1, 3)
            self.along(3)
            self.across(3, 0)

        def end(self, a):
            self.wait(STEPS[a], 2, 0, 6 + 4 * a)
            self.wait(STEPS[a], 2, 1, 7 + 4 * a)
            self.across(a, 3)

        def sibling(self):
            for a in range(4):
                for b in range(4):
                    self.wait(STEPS[a], STEPS[b], None, 20 + 4 * a + b, 1 - c)

    gf = Gather(F, fs, fr)
    gt = Gather(T, ts, tr)

    gf.first()
    for k in (1, 2, 3):
        mine = F.at[pl.ds(SLAB + g * ROWS, ROWS)]
        send(feat, mine, zs.at[k - 1], zr.at[k - 1], zed(k))
        send(pos, POS.at[g], zs.at[k + 2], zr.at[k + 2], zed(k))
    gf.second()
    gf.turn(0)
    gf.third()
    gf.turn(1)
    gf.turn(2)
    gf.turn(3)
    gt.first()
    for a in range(4):
        gf.end(a)
    gt.second()
    gf.sibling()

    def from_zed(k):
        return (g - k + 4) % 4

    for k in (1, 2, 3):
        o = from_zed(k)
        landed(F.at[pl.ds(SLAB + o * ROWS, ROWS)], zs.at[k - 1], zr.at[k - 1])

    for r in range(2):
        rows = pl.ds(r * BLOCK, BLOCK)
        agg = jnp.zeros((BLOCK, D), F32)
        for k in range(K):
            b = cols[r, k]
            device = b // 2
            group, domain = device // N_DOM, device % N_DOM
            at = jnp.where(group == g, domain * 2 + b % 2, SLAB // BLOCK + group * 2 + b % 2)
            agg = agg + dot(adj[rows, k * BLOCK:(k + 1) * BLOCK], F[pl.ds(at * BLOCK, BLOCK), :])
        high = agg.astype(BF)
        low = (agg - high.astype(F32)).astype(BF)
        AGG[pl.ds(c * ROWS + r * BLOCK, BLOCK), :] = high
        pre = (
            dot(feat[rows, :], self_w[...])
            + (dot(high, nbr_w[...]) + dot(low, nbr_w[...]))
            + bias[...]
        )
        hidden = jnp.maximum(pre, 0.0)
        HID[rows, :] = hidden
        emb[rows, :] = hidden.astype(BF)
        Q[g, rows, :] = (hidden * rms_scale(hidden)).astype(BF)

    for k in (1, 2, 3):
        send(Q.at[g], Q.at[g], zs.at[k + 5], zr.at[k + 5], zed(k))
    agg_own = AGG.at[pl.ds(c * ROWS, ROWS)]
    send(agg_own, agg_own, ms.at[0], mr.at[0], sib)

    gt.turn(0)
    gt.third()
    for a in (1, 2, 3):
        gt.turn(a)
    for a in range(4):
        gt.end(a)
    gt.sibling()
    for k in (1, 2, 3):
        o = from_zed(k)
        landed(POS.at[o], zs.at[k + 2], zr.at[k + 2])

    lanes = lax.broadcasted_iota(jnp.int32, (ROWS, CHUNK), 1)

    for k in (1, 2, 3, 0):
        o = (g + k) % 4
        if k:
            landed(Q.at[o], zs.at[9 - k], zr.at[9 - k])
        WACC[...] = jnp.zeros_like(WACC)
        TACC[...] = jnp.zeros_like(TACC)

        @pl.loop(0, SLAB // CHUNK)
        def _(n, o=o):
            part = T[pl.ds(n * CHUNK, CHUNK), :]
            e = jnp.exp2(dot_nt(Q[o], part) * (SCALE * LOG2E))
            tot = TACC[...]
            for m in range(CHUNK // 128):
                tot = tot + e[:, m * 128:(m + 1) * 128]
            TACC[...] = tot
            where = POS[o] - (g * SLAB + n * CHUNK)
            hot = jnp.concatenate([where] * (CHUNK // 128), axis=1) == lanes
            hot = hot.astype(F32).astype(BF)
            WACC[...] += dot(jnp.concatenate([e.astype(BF), hot], axis=0), part)

        if k:
            WP_S[k - 1] = WACC[...].astype(BF)
            TOT_S[k - 1] = TACC[...]
            send(WP_S.at[k - 1], WP_R.at[k - 1], zs.at[k + 8], zr.at[k + 8], zed(k))
            send(TOT_S.at[k - 1], TOT_R.at[k - 1], zs.at[k + 11], zr.at[k + 11], zed(k))

    for k in (1, 2, 3):
        landed(WP_R.at[k - 1], zs.at[k + 8], zr.at[k + 8])
        landed(TOT_R.at[k - 1], zs.at[k + 11], zr.at[k + 11])

    weighted = WACC[0:ROWS, :]
    picked = WACC[ROWS:2 * ROWS, :]
    lanes_total = TACC[...]
    for k in range(3):
        weighted = weighted + WP_R[k, 0:ROWS, :].astype(F32)
        picked = picked + WP_R[k, ROWS:2 * ROWS, :].astype(F32)
        lanes_total = lanes_total + TOT_R[k]
    totals = jnp.sum(lanes_total, axis=1, keepdims=True)
    pos_logit = jnp.sum(Q[g].astype(F32) * picked, axis=1, keepdims=True) * SCALE
    loss = jnp.sum(jnp.log(totals) - pos_logit, axis=0, keepdims=True)
    hidden = HID[...]
    scale_rows = rms_scale(hidden)
    normed = hidden * scale_rows
    unit = SCALE * (weighted / totals - picked)
    back = scale_rows * (unit - normed * jnp.mean(unit * normed, axis=1, keepdims=True))
    grad_pre = jnp.where(hidden > 0, back, 0.0)
    G[pl.ds(c * ROWS, ROWS), :] = grad_pre.astype(BF)
    g_own = G.at[pl.ds(c * ROWS, ROWS)]
    send(g_own, g_own, ms.at[1], mr.at[1], sib)

    bias_sum = jnp.sum(grad_pre, axis=0, keepdims=True)
    parts = [bias_sum[:, m * 128:(m + 1) * 128] for m in range(4)]
    parts.append(jnp.broadcast_to(loss, (1, 128)))
    parts.append(jnp.zeros((3, 128), F32))
    value = jnp.concatenate(parts, axis=0)

    def split(v):
        high = v.astype(BF).astype(F32)
        return jnp.concatenate([high, v - high], axis=0).astype(BF)

    def join(pair):
        return pair[0:8, :] + pair[8:16, :]

    sib_rows = pl.ds((1 - c) * ROWS, ROWS)
    landed(AGG.at[sib_rows], ms.at[0], mr.at[0])
    landed(G.at[sib_rows], ms.at[1], mr.at[1])
    pair = F[pl.ds((d // 2) * 2 * ROWS, 2 * ROWS), :]
    left = jnp.where(c == 0, pair, AGG[...])
    extra = split(value)
    for m in range(4):
        SA[m, 0:D, :] = dot_tn(left, G[:, m * 128:(m + 1) * 128]).astype(BF)
        SA[m, D:D + 16, :] = extra

    def exchange(S, R, at, ring, base, rows):
        for k in (1, 2, 3):
            send(S.at[(at + k) % 4], R.at[k - 1], gs.at[base + k], gr.at[base + k], ring(k))
        for k in (1, 2, 3):
            landed(R.at[k - 1], gs.at[base + k], gr.at[base + k])
        total = S[at].astype(F32)
        for k in range(3):
            total = total + R[k].astype(F32)
        return total[0:rows, :], join(total[rows:rows + 16, :])

    total, value = exchange(SA, RA, pi, prim, 0, D)
    extra = split(value)
    for m in range(4):
        SB[m, 0:192, :] = total[m * 192:(m + 1) * 192, :].astype(BF)
        SB[m, 192:208, :] = extra
    total, value = exchange(SB, RB, si, sec, 3, 192)
    extra = split(value)
    for m in range(4):
        SC[m, 0:48, :] = total[m * 48:(m + 1) * 48, :].astype(BF)
        SC[m, 48:64, :] = extra
    total, value = exchange(SC, RC, g, zed, 6, 48)

    EX[c] = split(value)
    send(EX.at[c], EX.at[c], ms.at[2], mr.at[2], sib)

    def spread(ring, base, row_of, rows):
        ref = grads.at[c, pl.ds(row_of(0), rows)]
        for k in (1, 2, 3):
            send(ref, ref, gs.at[base + k], gr.at[base + k], ring(k))
        for k in (1, 2, 3):
            landed(grads.at[c, pl.ds(row_of(-k), rows)], gs.at[base + k], gr.at[base + k])

    def at(p, s, z):
        return ((pi + p + 4) % 4) * 768 + ((si + s + 4) % 4) * 192 + ((g + z + 4) % 4) * 48

    grads[c, pl.ds(at(0, 0, 0), 48), :] = total.astype(BF)
    spread(zed, 9, lambda k: at(0, 0, k), 48)
    spread(sec, 12, lambda k: pi * 768 + ((si + k + 4) % 4) * 192, 192)

    def block(k, cc=None):
        which = c if cc is None else cc
        index = x * (1 - which) + y * which
        return grads.at[which, pl.ds(((index + k + 4) % 4) * 768, 768)]

    for k in (1, 2, 3):
        send(block(0), block(0), gs.at[15 + k], gr.at[15 + k], prim(k))
    send(block(0), block(0), ms.at[3], mr.at[3], sib)
    for k in (1, 2, 3):
        landed(block(-k), gs.at[15 + k], gr.at[15 + k])
        send(block(-k), block(-k), ms.at[3 + k], mr.at[3 + k], sib)
    landed(EX.at[1 - c], ms.at[2], mr.at[2])
    extra_out[...] = join(EX[0].astype(F32)) + join(EX[1].astype(F32))
    for k in range(4):
        landed(block(-k, 1 - c), ms.at[3 + k], mr.at[3 + k])
    for cp in pending:
        cp.wait_send()


def shards(features, text_embed, adjacency, block_cols, positive, self_weight, nbr_weight, hidden_bias):
    pos = jnp.broadcast_to(positive[:, None], (ROWS, 128))
    vmem = pl.BlockSpec(memory_space=pltpu.VMEM)
    smem = pl.BlockSpec(memory_space=pltpu.SMEM)
    dma = pltpu.SemaphoreType.DMA
    emb, grads, extra = pl.pallas_call(
        kernel,
        name="step",
        out_shape=(
            jax.ShapeDtypeStruct((ROWS, H), BF),
            jax.ShapeDtypeStruct((2, 4 * D, 128), BF),
            jax.ShapeDtypeStruct((8, 128), F32),
        ),
        in_specs=[vmem, vmem, vmem, smem, vmem, vmem, vmem, vmem],
        out_specs=(vmem, vmem, vmem),
        scratch_shapes=[
            pltpu.VMEM((SLAB + N_GRP * ROWS, D), BF),
            pltpu.VMEM((SLAB, H), BF),
            pltpu.VMEM((N_GRP, ROWS, H), BF),
            pltpu.VMEM((N_GRP, ROWS, 128), jnp.int32),
            pltpu.VMEM((2 * ROWS, D), BF),
            pltpu.VMEM((ROWS, H), F32),
            pltpu.VMEM((2 * ROWS, H), BF),
            pltpu.VMEM((2 * ROWS, H), F32),
            pltpu.VMEM((ROWS, 128), F32),
            pltpu.VMEM((3, 2 * ROWS, H), BF),
            pltpu.VMEM((3, 2 * ROWS, H), BF),
            pltpu.VMEM((3, ROWS, 128), F32),
            pltpu.VMEM((3, ROWS, 128), F32),
            pltpu.VMEM((4, D + 16, 128), BF),
            pltpu.VMEM((3, D + 16, 128), BF),
            pltpu.VMEM((4, 208, 128), BF),
            pltpu.VMEM((3, 208, 128), BF),
            pltpu.VMEM((4, 64, 128), BF),
            pltpu.VMEM((3, 64, 128), BF),
            pltpu.VMEM((2, 16, 128), BF),
            dma((GATHER_SEMS,)), dma((GATHER_SEMS,)),
            dma((GATHER_SEMS,)), dma((GATHER_SEMS,)),
            dma((15,)), dma((15,)),
            dma((7,)), dma((7,)),
            dma((19,)), dma((19,)),
        ],
        compiler_params=pltpu.CompilerParams(
            collective_id=0, has_side_effects=True, vmem_limit_bytes=56 * 2**20
        ),
        cost_estimate=pl.CostEstimate(
            flops=30 * 10**9, bytes_accessed=8 * 2**20, transcendentals=8 * 2**20
        ),
    )(
        features, text_embed, adjacency, block_cols, pos, self_weight, nbr_weight,
        hidden_bias.reshape(1, H),
    )
    wide = grads.reshape(2, 4, D, 128).transpose(0, 2, 1, 3).reshape(2, D, H).astype(F32)
    return emb, extra[4, 0] / NODES, wide[0], wide[1], extra[0:4].reshape(H)


def solution(mesh):
    rows = P(("grp", "dom"), None)
    return jax.shard_map(
        shards,
        mesh=mesh,
        in_specs=(rows, rows, rows, rows, P(("grp", "dom")), P(), P(), P()),
        out_specs=(rows, P(), P(), P(), P()),
        check_vma=False,
    )
```

time: 442 us -> 167 us (0.38)
  waiting for transfers between devices: 263 us -> 0 us
  Pallas kernels: 0 us -> 154 us
  blocking collectives: 64.8 us -> 0 us
  matrix products: 64 us -> 0 us
  other arithmetic: 20.5 us -> 1.61 us
  between operations: 15.7 us -> 2.46 us
  local copies, waits for them, and re-layouts: 13.4 us -> 8.8 us
    all_gather x3 -> x0, waiting for transfers between devices: 174 us -> none  [the longest x1 81.8 us: shards(): block_text = lax.all_gather(text_unit, ('grp', 'dom'), axis=0, tiled=True)]
    pallas_call x0 -> x1, Pallas kernels: none -> 154 us  [shards(): pl.pallas_call(kernel, name='step', out_shape=(jax.ShapeDtypeStruct((ROWS...]
    psum x1 -> x0, waiting for transfers between devices: 87 us -> none  [shards(): lax.psum((grad_self, grad_nbr, grad_bias, loss_part), ('grp', 'dom'))]
    psum x1 -> x0, blocking collectives: 64.8 us -> none  [shards(): lax.psum((grad_self, grad_nbr, grad_bias, loss_part), ('grp', 'dom'))]
    dot_general x8 -> x0, matrix products: 64 us -> none  [the longest x1 20.4 us: shards(): jnp.dot(exponent.astype(jnp.bfloat16), block_text, preferred_element_type...]
    concatenate x1 -> x0, other arithmetic: 16 us -> none  [shards(): jnp.concatenate([gathered_group, gathered_cross], axis=0)]
    gather x1 -> x0, local copies, waits for them, and re-layouts: 7.54 us -> none  [shards(): panel_table[lookup_position]]
    unnamed x18 -> x3, local copies, waits for them, and re-layouts: 5.73 us -> 0.71 us
  transfers between devices with their start and end apart: 4 -> 0, of which waited for: 4 -> 0; matrix products, arithmetic and copies ran while one was open for 7% -> 0% of each run, Pallas kernels for 0% -> 0%
where the time goes in v1:
time: 167 us
  Pallas kernels  154 us (92%)
  local copies, waits for them, and re-layouts  8.8 us (5%)
  between operations  2.46 us (1%)
    pallas_call x1, Pallas kernels, shards(): pl.pallas_call(kernel, name='step', out_shape=(jax.ShapeDtypeStruct((ROWS...  154 us
    slice x4, local copies, waits for them, and re-layouts, shards(): return (emb, extra[4, 0] / NODES, wide[0], wide[1], extra[0:4].reshape(H))  3.43 us

profile of v1, /device:TPU:1, one launch (start us, length us, event | category | flops | bytes accessed | tf_op | source)
XLA Modules:
  0.0 166.7 jit_solution(17922763658455751376)
XLA Ops:
  0.6 1.4 broadcast_in_dim.2.pos
  2.1 153.9 %step.1 = (bf16[256,512]{1,0:T(8,128)(2,1)}, bf16[2,3072,128]{2,1,0:T(8,128)(2,1)}, f32[8,128]{1,0:T(8,128)}) custom-call(bf16[256,768]{1,0:T(8,128)(2,1)} %feat.1, bf16[256,512]{1,0:T(8,128)(2,1)} %text.1, bf16[256,1024]{1,0:T(8,128)(2,1)} %adj.1, s32[2,8]{1,0:T(2,128)} %cols.1, s32[256,128]{1,0:T(8,128)} %broadcast_in_dim.2.pos, bf16[768,512]{1,0:T(8,128)(2,1)} %self_w.1, ...), custom_call_target="tpu_custom_call" | custom-call | flops 30000001024 | bytes 8388608 | tf_op jit(solution)/shard_map/step/pallas_call | solution.py:378
  155.9 1.2 slice.14
  157.8 1.3 slice_bitcast_fusion
  159.0 1.6 convert_bitcast_fusion
  160.7 0.2 fusion
  160.9 1.0 copy.14
  161.9 1.0 copy.13
  162.9 0.0 copy-start
  162.9 2.0 %copy_bitcast_fusion = (f32[768,512]{1,0:T(8,128)}, f32[768,512]{1,0:T(8,128)}) fusion(f32[96,8,4,128]{3,2,1,0:T(4,128)S(1)} %bitcast.16, f32[96,8,4,128]{3,2,1,0:T(4,128)S(1)} %bitcast.17), kind=kLoop, calls=%fused_computation.1 | loop fusion | bytes 6291456 | tf_op jit(solution)/shard_map/squeeze | solution.py:426
  164.9 0.0 copy-done
  164.9 0.7 copy.20
Async XLA Ops:
  162.9 2.0 %copy-start = (bf16[256,512]{1,0:T(8,128)(2,1)S(1)}, bf16[256,512]{1,0:T(8,128)(2,1)}, u32[]{:S(2)}) copy-start(bf16[256,512]{1,0:T(8,128)(2,1)} %get-tuple-element.20) | copy-start | bytes 786436

commit v2 on v1

v2 whole, which is shorter than its diff:
```python
import functools

import jax
import jax.numpy as jnp
from jax import lax
from jax.experimental import pallas as pl
from jax.experimental.pallas import tpu as pltpu
from jax.sharding import PartitionSpec as P

MESH = pl.DeviceIdType.MESH
D = 768
H = 512
BLOCK = 128
K = 8
ROWS = 256
HALF = 128
N_GRP = 4
N_DOM = 32
NODES = 32768
SLAB = N_DOM * ROWS
CHUNK = 2048

EPS = 1e-05
SCALE = 10.0 / H
LOG2E = 1.4426950408889634

BF = jnp.bfloat16
F32 = jnp.float32

ORDER = (
    (-1, 0, 0), (1, 0, 1), (-1, 0, 1), (1, 0, 0), (0, -1, 0), (0, 1, 0), (0, -1, 1), (0, 1, 1),
    (2, 0, 0), (-1, 1, 0), (-1, -1, 0), (2, 0, 1), (1, -1, 1), (1, 1, 1), (-1, -1, 1), (-1, 1, 1),
    (1, -1, 0), (1, 1, 0), (0, 2, 0), (0, 2, 1), (2, -1, 0), (2, 1, 0), (-1, 2, 0), (2, 1, 1),
    (2, -1, 1), (1, 2, 1), (-1, 2, 1), (1, 2, 0), (2, 2, 0), (2, 2, 1),
)
SHARDS = (
    (0, 0), (-1, 0), (1, 0), (0, -1), (0, 1), (2, 0), (-1, -1), (-1, 1),
    (1, -1), (1, 1), (0, 2), (2, -1), (2, 1), (-1, 2), (1, 2), (2, 2),
)
UNITS = (7, 15, 24, 29)
GATHER_SEMS = len(ORDER) + len(SHARDS)


def rms_scale(values):
    return lax.rsqrt(jnp.mean(values * values, axis=1, keepdims=True) + EPS)


def dot(a, b):
    return jnp.dot(a, b, preferred_element_type=F32)


def dot_nt(a, b):
    return lax.dot_general(a, b, (((1,), (1,)), ((), ())), preferred_element_type=F32)


def column(row):
    return jnp.transpose(jnp.broadcast_to(row, (128, ROWS)))


def kernel(
    feat, text, adj_h, cols, pos, self_h, nbr_h, bias,
    emb, grads, extra_out,
    F, T, Q, POS, PCOL, AGG, HID, G, LT, W_OWN, T_OWN, WACC, TACC, PACC, W_S, W_R, P_R, TOT_S, TOT_R,
    SA, RA, SB, RB, SC, RC, EX, adj, self_w, nbr_w,
    fs, fr, ts, tr, zs, zr, ms, mr, gs, gr, ls,
):
    g = lax.axis_index("grp")
    d = lax.axis_index("dom")
    c = d % 2
    x = (d // 2) % 4
    y = d // 8
    loads = [
        pltpu.make_async_copy(src, dst, ls.at[n])
        for n, (src, dst) in enumerate(((adj_h, adj), (self_h, self_w), (nbr_h, nbr_w)))
    ]
    for load in loads:
        load.start()

    def dom_at(i, j, cc):
        ux, uy = 1 - cc, cc
        ax = (x + i * ux + j * uy + 4) % 4
        ay = (y + i * uy + j * ux + 4) % 4
        return (ay * 4 + ax) * 2 + cc

    def prim(k):
        return (g, dom_at(k, 0, c))

    def sec(k):
        return (g, dom_at(0, k, c))

    def zed(k):
        return ((g + k) % 4, d)

    sib = (g, d + 1 - 2 * c)
    pi = x * (1 - c) + y * c
    si = x * c + y * (1 - c)

    def rcopy(src, dst, ssem, rsem, dev):
        return pltpu.make_async_remote_copy(
            src_ref=src, dst_ref=dst, send_sem=ssem, recv_sem=rsem,
            device_id=dev, device_id_type=MESH,
        )

    pending = []

    def send(src, dst, ssem, rsem, dev):
        cp = rcopy(src, dst, ssem, rsem, dev)
        cp.start()
        pending.append(cp)

    def landed(region, ssem, rsem):
        rcopy(region, region, ssem, rsem, sib).wait_recv()

    barrier = pltpu.get_barrier_semaphore()
    partners = [sib] + [f(k) for f in (prim, sec, zed) for k in (1, 2, 3)]
    for dev in partners:
        pl.semaphore_signal(barrier, inc=1, device_id=dev, device_id_type=MESH)

    own = pl.ds(d * ROWS, ROWS)
    F[own, :] = feat[...]
    tw = text[...].astype(F32)
    T[own, :] = (tw * rms_scale(tw)).astype(BF)
    POS[g] = jnp.broadcast_to(pos[...].astype(F32), (8, ROWS))
    pl.semaphore_wait(barrier, len(partners))

    class Gather:
        def __init__(self, tab, ssem, rsem):
            self.tab, self.ss, self.rs = tab, ssem, rsem

        def shard(self, i, j, cc, half=None):
            base = dom_at(i, j, cc) * ROWS
            if half is None:
                return self.tab.at[pl.ds(base, ROWS)]
            return self.tab.at[pl.ds(base + half * HALF, HALF)]

        def send(self, key, to, dev):
            ref = self.shard(key[0], key[1], c, key[2])
            k = ORDER.index(to + (key[2],))
            send(ref, ref, self.ss.at[k], self.rs.at[k], dev)

        def across(self, i, j):
            ref = self.shard(i, j, c)
            k = len(ORDER) + SHARDS.index((i, j))
            send(ref, ref, self.ss.at[k], self.rs.at[k], sib)

        def along(self, i, h):
            self.send((i, 0, h), (i, -1), sec(1))
            self.send((i, 0, h), (i, 1), sec(-1))

        def start(self):
            self.send((0, 0, 0), (-1, 0), prim(1))
            self.send((0, 0, 1), (1, 0), prim(-1))
            self.send((0, 0, 1), (-1, 0), prim(1))
            self.send((0, 0, 0), (1, 0), prim(-1))
            self.along(0, 0)
            self.along(0, 1)
            self.across(0, 0)
            self.here = set()

        def step(self, n):
            i, j, h = key = ORDER[n]
            landed(self.shard(i, j, c, h), self.ss.at[n], self.rs.at[n])
            if key == (-1, 0, 0):
                self.send(key, (2, 0), prim(1))
            if key == (1, 0, 1):
                self.send(key, (2, 0), prim(-1))
            if j == 0:
                self.along(i, h)
            if j == -1 and h == 0:
                self.send(key, (i, 2), sec(1))
            if j == 1 and h == 1:
                self.send(key, (i, 2), sec(-1))
            if (i, j) in self.here:
                self.across(i, j)
            self.here.add((i, j))

        def sibling(self, i, j):
            k = len(ORDER) + SHARDS.index((i, j))
            landed(self.shard(i, j, 1 - c), self.ss.at[k], self.rs.at[k])

    gf = Gather(F, fs, fr)
    gt = Gather(T, ts, tr)

    gf.start()
    for k in (1, 2, 3):
        mine = F.at[pl.ds(SLAB + g * ROWS, ROWS)]
        send(feat, mine, zs.at[k - 1], zr.at[k - 1], zed(k))
        send(POS.at[g], POS.at[g], zs.at[k + 2], zr.at[k + 2], zed(k))
    for n in range(25):
        gf.step(n)
    gt.start()
    for n in range(25, 30):
        gf.step(n)
    for n in range(2):
        gt.step(n)
    for i, j in SHARDS:
        gf.sibling(i, j)

    def from_zed(k):
        return (g - k + 4) % 4

    for k in (1, 2, 3):
        o = from_zed(k)
        landed(F.at[pl.ds(SLAB + o * ROWS, ROWS)], zs.at[k - 1], zr.at[k - 1])

    for load in loads:
        load.wait()
    for r in range(2):
        rows = pl.ds(r * BLOCK, BLOCK)
        agg = jnp.zeros((BLOCK, D), F32)
        for k in range(K):
            b = cols[r, k]
            device = b // 2
            group, domain = device // N_DOM, device % N_DOM
            at = jnp.where(group == g, domain * 2 + b % 2, SLAB // BLOCK + group * 2 + b % 2)
            agg = agg + dot(adj[rows, k * BLOCK:(k + 1) * BLOCK], F[pl.ds(at * BLOCK, BLOCK), :])
        high = agg.astype(BF)
        low = (agg - high.astype(F32)).astype(BF)
        AGG[pl.ds(c * ROWS + r * BLOCK, BLOCK), :] = high
        pre = (
            dot(feat[rows, :], self_w[...])
            + (dot(high, nbr_w[...]) + dot(low, nbr_w[...]))
            + bias[...]
        )
        hidden = jnp.maximum(pre, 0.0)
        HID[rows, :] = hidden
        emb[rows, :] = hidden.astype(BF)
        Q[g, rows, :] = (hidden * rms_scale(hidden)).astype(BF)

    for k in (1, 2, 3):
        send(Q.at[g], Q.at[g], zs.at[k + 5], zr.at[k + 5], zed(k))
    agg_own = AGG.at[pl.ds(c * ROWS, ROWS)]
    send(agg_own, agg_own, ms.at[0], mr.at[0], sib)

    for k in (1, 2, 3):
        o = from_zed(k)
        landed(POS.at[o], zs.at[k + 2], zr.at[k + 2])
    for o in range(N_GRP):
        PCOL[o * ROWS:(o + 1) * ROWS, :] = column(POS[o, 0:1, :])
    PACC[...] = jnp.zeros_like(PACC)
    lanes = lax.broadcasted_iota(jnp.int32, (N_GRP * ROWS, 128), 1).astype(F32)

    def contrast(o, part, WACC, TACC):
        e = jnp.exp2(dot_nt(Q[o], part) * (SCALE * LOG2E))
        tot = TACC[...]
        for m in range(part.shape[0] // 128):
            tot = tot + e[:, m * 128:(m + 1) * 128]
        TACC[...] = tot
        WACC[...] += dot(e.astype(BF), part)

    def clear(WACC, TACC):
        WACC[...] = jnp.zeros_like(WACC)
        TACC[...] = jnp.zeros_like(TACC)

    def pick(doms, part):
        hot = []
        for dom in doms:
            for m in range(ROWS // 128):
                at = (g * SLAB + dom * ROWS + m * 128).astype(F32)
                hot.append(jnp.where(PCOL[...] - at == lanes, 1.0, 0.0).astype(BF))
        PACC[...] += dot(jnp.concatenate(hot, axis=1), part).astype(BF)

    def gathered(doms):
        return jnp.concatenate([T[pl.ds(dom * ROWS, ROWS), :] for dom in doms], axis=0)

    clear(W_OWN, T_OWN)
    sib_rows = pl.ds((1 - c) * ROWS, ROWS)
    landed(AGG.at[sib_rows], ms.at[0], mr.at[0])
    pair = F[pl.ds((d // 2) * 2 * ROWS, 2 * ROWS), :]
    LT[...] = jnp.transpose(jnp.where(c == 0, pair, AGG[...]))
    done = 2
    for u, last in enumerate(UNITS):
        while done <= last:
            gt.step(done)
            done += 1
        group = SHARDS[4 * u:4 * u + 4]
        for cc in (c, 1 - c):
            if cc is not c:
                for i, j in group:
                    gt.sibling(i, j)
            doms = [dom_at(i, j, cc) for i, j in group]
            part = gathered(doms)
            pick(doms, part)
            contrast(g, part, W_OWN, T_OWN)

    for k in (1, 2, 3):
        o = (g + k) % 4
        ref = PACC.at[pl.ds(o * ROWS, ROWS)]
        send(ref, P_R.at[k - 1], zs.at[k + 8], zr.at[k + 8], zed(k))
    for k in (1, 2, 3):
        o = (g + k) % 4
        landed(Q.at[o], zs.at[9 - k], zr.at[9 - k])
        clear(WACC, TACC)

        @pl.loop(0, SLAB // CHUNK)
        def _(n, o=o):
            contrast(o, T[pl.ds(n * CHUNK, CHUNK), :], WACC, TACC)

        W_S[k - 1] = WACC[...].astype(BF)
        TOT_S[k - 1] = lax.dot_general(
            jnp.ones((8, 128), F32), TACC[...], (((1,), (1,)), ((), ())),
            precision=lax.Precision.HIGHEST, preferred_element_type=F32,
        )
        send(W_S.at[k - 1], W_R.at[k - 1], zs.at[k + 11], zr.at[k + 11], zed(k))
        send(TOT_S.at[k - 1], TOT_R.at[k - 1], zs.at[k + 14], zr.at[k + 14], zed(k))
    for k in (1, 2, 3):
        landed(P_R.at[k - 1], zs.at[k + 8], zr.at[k + 8])
        landed(W_R.at[k - 1], zs.at[k + 11], zr.at[k + 11])
        landed(TOT_R.at[k - 1], zs.at[k + 14], zr.at[k + 14])

    weighted = W_OWN[...]
    picked = PACC[pl.ds(g * ROWS, ROWS), :].astype(F32)
    for k in range(3):
        weighted = weighted + W_R[k].astype(F32)
        picked = picked + P_R[k].astype(F32)
    totals = jnp.sum(T_OWN[...], axis=1, keepdims=True)
    totals = totals + column((TOT_R[0] + TOT_R[1] + TOT_R[2])[0:1, :])[:, 0:1]
    pos_logit = jnp.sum(Q[g].astype(F32) * picked, axis=1, keepdims=True) * SCALE
    loss = jnp.sum(jnp.log(totals) - pos_logit, axis=0, keepdims=True)
    hidden = HID[...]
    scale_rows = rms_scale(hidden)
    normed = hidden * scale_rows
    unit = SCALE * (weighted / totals - picked)
    back = scale_rows * (unit - normed * jnp.mean(unit * normed, axis=1, keepdims=True))
    grad_pre = jnp.where(hidden > 0, back, 0.0)
    G[pl.ds(c * ROWS, ROWS), :] = grad_pre.astype(BF)
    g_own = G.at[pl.ds(c * ROWS, ROWS)]
    send(g_own, g_own, ms.at[1], mr.at[1], sib)

    bias_sum = jnp.sum(grad_pre, axis=0, keepdims=True)
    parts = [bias_sum[:, m * 128:(m + 1) * 128] for m in range(4)]
    parts.append(jnp.broadcast_to(loss, (1, 128)))
    parts.append(jnp.zeros((3, 128), F32))
    value = jnp.concatenate(parts, axis=0)

    def split(v):
        high = v.astype(BF).astype(F32)
        return jnp.concatenate([high, v - high], axis=0).astype(BF)

    def join(pair):
        return pair[0:8, :] + pair[8:16, :]

    landed(G.at[sib_rows], ms.at[1], mr.at[1])
    extra = split(value)
    grad = dot(LT[...], G[...]).astype(BF)
    for m in range(4):
        SA[m, 0:D, :] = grad[:, m * 128:(m + 1) * 128]
        SA[m, D:D + 16, :] = extra

    def exchange(S, R, at, ring, base, rows):
        for k in (1, 2, 3):
            send(S.at[(at + k) % 4], R.at[k - 1], gs.at[base + k], gr.at[base + k], ring(k))
        for k in (1, 2, 3):
            landed(R.at[k - 1], gs.at[base + k], gr.at[base + k])
        total = S[at].astype(F32)
        for k in range(3):
            total = total + R[k].astype(F32)
        return total[0:rows, :], join(total[rows:rows + 16, :])

    total, value = exchange(SA, RA, pi, prim, 0, D)
    extra = split(value)
    for m in range(4):
        SB[m, 0:192, :] = total[m * 192:(m + 1) * 192, :].astype(BF)
        SB[m, 192:208, :] = extra
    total, value = exchange(SB, RB, si, sec, 3, 192)
    extra = split(value)
    for m in range(4):
        SC[m, 0:48, :] = total[m * 48:(m + 1) * 48, :]
        SC[m, 48:64, :] = extra.astype(F32)
    total, value = exchange(SC, RC, g, zed, 6, 48)

    EX[c] = split(value)
    send(EX.at[c], EX.at[c], ms.at[2], mr.at[2], sib)

    def spread(ring, base, row_of, rows):
        ref = grads.at[c, pl.ds(row_of(0), rows)]
        for k in (1, 2, 3):
            send(ref, ref, gs.at[base + k], gr.at[base + k], ring(k))
        for k in (1, 2, 3):
            landed(grads.at[c, pl.ds(row_of(-k), rows)], gs.at[base + k], gr.at[base + k])

    def at(p, s, z):
        return ((pi + p + 4) % 4) * 768 + ((si + s + 4) % 4) * 192 + ((g + z + 4) % 4) * 48

    grads[c, pl.ds(at(0, 0, 0), 48), :] = total.astype(BF)
    spread(zed, 9, lambda k: at(0, 0, k), 48)
    spread(sec, 12, lambda k: pi * 768 + ((si + k + 4) % 4) * 192, 192)

    def block(k, cc=None):
        which = c if cc is None else cc
        index = x * (1 - which) + y * which
        return grads.at[which, pl.ds(((index + k + 4) % 4) * 768, 768)]

    for k in (1, 2, 3):
        send(block(0), block(0), gs.at[15 + k], gr.at[15 + k], prim(k))
    send(block(0), block(0), ms.at[3], mr.at[3], sib)
    for k in (1, 2, 3):
        landed(block(-k), gs.at[15 + k], gr.at[15 + k])
        send(block(-k), block(-k), ms.at[3 + k], mr.at[3 + k], sib)
    landed(EX.at[1 - c], ms.at[2], mr.at[2])
    extra_out[...] = join(EX[0].astype(F32)) + join(EX[1].astype(F32))
    for k in range(4):
        landed(block(-k, 1 - c), ms.at[3 + k], mr.at[3 + k])
    for cp in pending:
        cp.wait_send()


def finish(emb_in, grads, extra, emb, loss, grad_self, grad_nbr, grad_bias):
    emb[...] = emb_in[...]
    loss[...] = extra[4:5, 0:1] * (1.0 / NODES)
    for m in range(4):
        at = slice(m * 128, (m + 1) * 128)
        grad_self[:, at] = grads[0, m * D:(m + 1) * D, :].astype(F32)
        grad_nbr[:, at] = grads[1, m * D:(m + 1) * D, :].astype(F32)
        grad_bias[:, at] = extra[m:m + 1, :]


def shards(features, text_embed, adjacency, block_cols, positive, self_weight, nbr_weight, hidden_bias):
    vmem = pl.BlockSpec(memory_space=pltpu.VMEM)
    smem = pl.BlockSpec(memory_space=pltpu.SMEM)
    hbm = pl.BlockSpec(memory_space=pl.ANY)
    dma = pltpu.SemaphoreType.DMA
    emb, grads, extra = pl.pallas_call(
        kernel,
        name="step",
        out_shape=(
            jax.ShapeDtypeStruct((ROWS, H), BF),
            jax.ShapeDtypeStruct((2, 4 * D, 128), BF),
            jax.ShapeDtypeStruct((8, 128), F32),
        ),
        in_specs=[vmem, vmem, hbm, smem, vmem, hbm, hbm, vmem],
        out_specs=(vmem, vmem, vmem),
        scratch_shapes=[
            pltpu.VMEM((SLAB + N_GRP * ROWS, D), BF),
            pltpu.VMEM((SLAB, H), BF),
            pltpu.VMEM((N_GRP, ROWS, H), BF),
            pltpu.VMEM((N_GRP, 8, ROWS), F32),
            pltpu.VMEM((N_GRP * ROWS, 128), F32),
            pltpu.VMEM((2 * ROWS, D), BF),
            pltpu.VMEM((ROWS, H), F32),
            pltpu.VMEM((2 * ROWS, H), BF),
            pltpu.VMEM((D, 2 * ROWS), BF),
            pltpu.VMEM((ROWS, H), F32),
            pltpu.VMEM((ROWS, 128), F32),
            pltpu.VMEM((ROWS, H), F32),
            pltpu.VMEM((ROWS, 128), F32),
            pltpu.VMEM((N_GRP * ROWS, H), BF),
            pltpu.VMEM((3, ROWS, H), BF),
            pltpu.VMEM((3, ROWS, H), BF),
            pltpu.VMEM((3, ROWS, H), BF),
            pltpu.VMEM((3, 8, ROWS), F32),
            pltpu.VMEM((3, 8, ROWS), F32),
            pltpu.VMEM((4, D + 16, 128), BF),
            pltpu.VMEM((3, D + 16, 128), BF),
            pltpu.VMEM((4, 208, 128), BF),
            pltpu.VMEM((3, 208, 128), BF),
            pltpu.VMEM((4, 64, 128), F32),
            pltpu.VMEM((3, 64, 128), F32),
            pltpu.VMEM((2, 16, 128), BF),
            pltpu.VMEM((ROWS, K * BLOCK), BF),
            pltpu.VMEM((D, H), BF),
            pltpu.VMEM((D, H), BF),
            dma((GATHER_SEMS,)), dma((GATHER_SEMS,)),
            dma((GATHER_SEMS,)), dma((GATHER_SEMS,)),
            dma((18,)), dma((18,)),
            dma((7,)), dma((7,)),
            dma((19,)), dma((19,)),
            dma((3,)),
        ],
        compiler_params=pltpu.CompilerParams(
            collective_id=0, has_side_effects=True, vmem_limit_bytes=56 * 2**20
        ),
        cost_estimate=pl.CostEstimate(
            flops=30 * 10**9, bytes_accessed=8 * 2**20, transcendentals=8 * 2**20
        ),
    )(
        features, text_embed, adjacency, block_cols, positive.reshape(1, ROWS), self_weight, nbr_weight,
        hidden_bias.reshape(1, H),
    )
    emb, loss, grad_self, grad_nbr, grad_bias = pl.pallas_call(
        finish,
        name="finish",
        out_shape=(
            jax.ShapeDtypeStruct((ROWS, H), BF),
            jax.ShapeDtypeStruct((1, 1), F32),
            jax.ShapeDtypeStruct((D, H), F32),
            jax.ShapeDtypeStruct((D, H), F32),
            jax.ShapeDtypeStruct((1, H), F32),
        ),
        in_specs=[vmem] * 3,
        out_specs=(vmem,) * 5,
    )(emb, grads, extra)
    return emb, loss.reshape(()), grad_self, grad_nbr, grad_bias.reshape(H)


def solution(mesh):
    rows = P(("grp", "dom"), None)
    return jax.shard_map(
        shards,
        mesh=mesh,
        in_specs=(rows, rows, rows, rows, P(("grp", "dom")), P(), P(), P()),
        out_specs=(rows, P(), P(), P(), P()),
        check_vma=False,
    )
```

time: 167 us -> 138 us (0.83)
  Pallas kernels: 154 us -> 138 us
  local copies, waits for them, and re-layouts: 8.8 us -> 0 us
  between operations: 2.46 us -> 0.64 us
    pallas_call x1, Pallas kernels: 154 us -> 134 us  [shards(): pl.pallas_call(kernel, name='step', out_shape=(jax.ShapeDtypeStruct((ROWS...]
    slice x4 -> x0, local copies, waits for them, and re-layouts: 3.43 us -> none  [shards(): return (emb, extra[4, 0] / NODES, wide[0], wide[1], extra[0:4].reshape(H))]
    pallas_call x0 -> x1, Pallas kernels: none -> 3.38 us  [shards(): pl.pallas_call(finish, name='finish', out_shape=(jax.ShapeDtypeStruct((RO...]
    squeeze x1 -> x0, local copies, waits for them, and re-layouts: 1.97 us -> none  [shards(): return (emb, extra[4, 0] / NODES, wide[0], wide[1], extra[0:4].reshape(H))]
where the time goes in v2:
time: 138 us
  Pallas kernels  138 us (100%)
    pallas_call x1, Pallas kernels, shards(): pl.pallas_call(kernel, name='step', out_shape=(jax.ShapeDtypeStruct((ROWS...  134 us
    pallas_call x1, Pallas kernels, shards(): pl.pallas_call(finish, name='finish', out_shape=(jax.ShapeDtypeStruct((RO...  3.38 us

profile of v2, /device:TPU:1, one launch (start us, length us, event | category | flops | bytes accessed | tf_op | source)
XLA Modules:
  0.0 138.2 jit_solution(3500388864315227320)
XLA Ops:
  0.6 134.2 %step.1 = (bf16[256,512]{1,0:T(8,128)(2,1)}, bf16[2,3072,128]{2,1,0:T(8,128)(2,1)}, f32[8,128]{1,0:T(8,128)}) custom-call(bf16[256,768]{1,0:T(8,128)(2,1)} %feat.1, bf16[256,512]{1,0:T(8,128)(2,1)} %text.1, bf16[256,1024]{1,0:T(8,128)(2,1)} %adj_h.1, s32[2,8]{1,0:T(2,128)} %cols.1, s32[1,256]{1,0:T(1,128)} %bitcast.6, bf16[768,512]{1,0:T(8,128)(2,1)} %self_h.1, ...), custom_call_target="tpu_custom_call" | custom-call | flops 30000001024 | bytes 8388608 | tf_op jit(solution)/shard_map/step/pallas_call | solution.py:423
  134.8 3.4 %finish.1 = (bf16[256,512]{1,0:T(8,128)(2,1)}, f32[1,1]{1,0:T(1,128)}, f32[768,512]{1,0:T(8,128)}, f32[768,512]{1,0:T(8,128)}, f32[1,512]{1,0:T(1,128)}) custom-call(bf16[256,512]{1,0:T(8,128)(2,1)} %get-tuple-element.13.emb_in, bf16[2,3072,128]{2,1,0:T(8,128)(2,1)} %get-tuple-element.14.grads, f32[8,128]{1,0:T(8,128)} %get-tuple-element.15.extra), custom_call_target="tpu_custom_call" | custom-call | tf_op jit(solution)/shard_map/finish/pallas_call | solution.py:480

commit v3 on v2

v3 whole, which is shorter than its diff:
```python
import jax
import jax.numpy as jnp
from jax import lax
from jax.experimental import pallas as pl
from jax.experimental.pallas import tpu as pltpu
from jax.sharding import PartitionSpec as P

MESH = pl.DeviceIdType.MESH
D = 768
H = 512
BLOCK = 128
K = 8
ROWS = 256
HALF = 128
N_GRP = 4
N_DOM = 32
NODES = 32768
SLAB = N_DOM * ROWS
WIDE = 1024
STRIP = 64

EPS = 1e-05
SCALE = 10.0 / H
LOG2E = 1.4426950408889634

BF = jnp.bfloat16
F32 = jnp.float32

ORDER = (
    (-1, 0, 0), (1, 0, 1), (-1, 0, 1), (1, 0, 0), (0, -1, 0), (0, 1, 0), (0, -1, 1), (0, 1, 1),
    (2, 0, 0), (-1, 1, 0), (-1, -1, 0), (2, 0, 1), (1, -1, 1), (1, 1, 1), (-1, -1, 1), (-1, 1, 1),
    (1, -1, 0), (1, 1, 0), (0, 2, 0), (0, 2, 1), (2, -1, 0), (2, 1, 0), (-1, 2, 0), (2, 1, 1),
    (2, -1, 1), (1, 2, 1), (-1, 2, 1), (1, 2, 0), (2, 2, 0), (2, 2, 1),
)
SHARDS = (
    (0, 0), (-1, 0), (1, 0), (0, -1), (0, 1), (2, 0), (-1, -1), (-1, 1),
    (1, -1), (1, 1), (0, 2), (2, -1), (2, 1), (-1, 2), (1, 2), (2, 2),
)
UNITS = (7, 15, 24, 29)
GATHER_SEMS = len(ORDER) + len(SHARDS)


def rms_scale(values):
    return lax.rsqrt(jnp.mean(values * values, axis=1, keepdims=True) + EPS)


def dot(a, b):
    return jnp.dot(a, b, preferred_element_type=F32)


def dot_nt(a, b):
    return lax.dot_general(a, b, (((1,), (1,)), ((), ())), preferred_element_type=F32)


def column(row):
    return jnp.transpose(jnp.broadcast_to(row, (128, ROWS)))


def lane_sums(a):
    return lax.dot_general(
        jnp.ones((8, 128), F32), a, (((1,), (1,)), ((), ())),
        precision=lax.Precision.HIGHEST, preferred_element_type=F32,
    )


def split(v):
    high = v.astype(BF).astype(F32)
    return jnp.concatenate([high, v - high], axis=0).astype(BF)


def join(pair):
    return pair[0:8, :] + pair[8:16, :]


def kernel(
    feat_h, text_h, adj_h, cols_h, pos_h, self_h, nbr_h, bias_h,
    emb_h, grads_h, extra_h,
    FE, T, Q, POS, PCOL, AGG, HID, G, LT, TACC, PACC, RT, W_S, W_R, W_O, TP_S, TP_R,
    SA, RA, SB, RB, EX, GR, XO,
    text, adj, cols, pos, self_w, nbr_w, bias, emb,
    fs, fr, ts, tr, zs, zr, ms, mr, gs, gr, ls,
):
    g = lax.axis_index("grp")
    d = lax.axis_index("dom")
    c = d % 2
    x = (d // 2) % 4
    y = d // 8

    def dom_at(i, j, cc):
        ux, uy = 1 - cc, cc
        ax = (x + i * ux + j * uy + 4) % 4
        ay = (y + i * uy + j * ux + 4) % 4
        return (ay * 4 + ax) * 2 + cc

    def prim(k):
        return (g, dom_at(k, 0, c))

    def sec(k):
        return (g, dom_at(0, k, c))

    def zed(k):
        return ((g + k) % 4, d)

    def wall(j, k):
        return ((g + k) % 4, dom_at(0, j, c))

    sib = (g, d + 1 - 2 * c)
    pi = x * (1 - c) + y * c
    si = x * c + y * (1 - c)
    F = FE.at[:, pl.ds(0, D)]

    barrier = pltpu.get_barrier_semaphore()
    across = [(j, k) for j in range(4) for k in range(4) if j or k]
    partners = [sib] + [prim(k) for k in (1, 2, 3)] + [wall(j, k) for j, k in across]
    for dev in partners:
        pl.semaphore_signal(barrier, inc=1, device_id=dev, device_id_type=MESH)

    own = pl.ds(d * ROWS, ROWS)
    loads = [
        pltpu.make_async_copy(src, dst, ls.at[n])
        for n, (src, dst) in enumerate((
            (text_h, text), (pos_h, pos), (feat_h, F.at[own]), (cols_h, cols), (bias_h, bias),
            (adj_h, adj), (self_h, self_w), (nbr_h, nbr_w),
        ))
    ]
    for load in loads:
        load.start()

    pending = []
    feature_sends = []

    def rcopy(src, dst, ssem, rsem, dev):
        return pltpu.make_async_remote_copy(
            src_ref=src, dst_ref=dst, send_sem=ssem, recv_sem=rsem,
            device_id=dev, device_id_type=MESH,
        )

    def send(src, dst, ssem, rsem, dev, kept=pending):
        cp = rcopy(src, dst, ssem, rsem, dev)
        cp.start()
        kept.append(cp)

    def landed(region, ssem, rsem):
        rcopy(region, region, ssem, rsem, sib).wait_recv()

    def drain(kept):
        for cp in kept:
            cp.wait_send()

    class Gather:
        def __init__(self, tab, ssem, rsem, kept):
            self.tab, self.ss, self.rs, self.kept = tab, ssem, rsem, kept
            self.here = set()
            self.done = 0

        def shard(self, i, j, cc, half=None):
            base = dom_at(i, j, cc) * ROWS
            if half is None:
                return self.tab.at[pl.ds(base, ROWS)]
            return self.tab.at[pl.ds(base + half * HALF, HALF)]

        def send(self, key, to, dev):
            ref = self.shard(key[0], key[1], c, key[2])
            k = ORDER.index(to + (key[2],))
            send(ref, ref, self.ss.at[k], self.rs.at[k], dev, self.kept)

        def across(self, i, j):
            ref = self.shard(i, j, c)
            k = len(ORDER) + SHARDS.index((i, j))
            send(ref, ref, self.ss.at[k], self.rs.at[k], sib, self.kept)

        def along(self, i, h):
            self.send((i, 0, h), (i, -1), sec(1))
            self.send((i, 0, h), (i, 1), sec(-1))

        def start(self):
            self.send((0, 0, 0), (-1, 0), prim(1))
            self.send((0, 0, 1), (1, 0), prim(-1))
            self.send((0, 0, 1), (-1, 0), prim(1))
            self.send((0, 0, 0), (1, 0), prim(-1))
            self.along(0, 0)
            self.along(0, 1)
            self.across(0, 0)

        def to(self, last):
            while self.done <= last:
                self.step(self.done)
                self.done += 1

        def step(self, n):
            i, j, h = key = ORDER[n]
            landed(self.shard(i, j, c, h), self.ss.at[n], self.rs.at[n])
            if key == (-1, 0, 0):
                self.send(key, (2, 0), prim(1))
            if key == (1, 0, 1):
                self.send(key, (2, 0), prim(-1))
            if j == 0:
                self.along(i, h)
            if j == -1 and h == 0:
                self.send(key, (i, 2), sec(1))
            if j == 1 and h == 1:
                self.send(key, (i, 2), sec(-1))
            if (i, j) in self.here:
                self.across(i, j)
            self.here.add((i, j))

        def sibling(self, i, j):
            k = len(ORDER) + SHARDS.index((i, j))
            landed(self.shard(i, j, 1 - c), self.ss.at[k], self.rs.at[k])

    gf = Gather(F, fs, fr, feature_sends)
    gt = Gather(T, ts, tr, pending)

    loads[0].wait()
    tw = text[...].astype(F32)
    T[own, :] = (tw * rms_scale(tw)).astype(BF)
    loads[1].wait()
    POS[g] = jnp.broadcast_to(pos[...].astype(F32), (8, ROWS))
    loads[2].wait()
    pl.semaphore_wait(barrier, len(partners))

    gf.start()
    mine = F.at[pl.ds(SLAB + g * ROWS, ROWS)]
    for k in (1, 3, 2):
        send(F.at[own], mine, zs.at[k - 1], zr.at[k - 1], zed(k), feature_sends)
        send(POS.at[g], POS.at[g], zs.at[k + 2], zr.at[k + 2], zed(k))
    gf.to(24)
    gt.start()
    gf.to(29)
    gt.to(3)
    for i, j in SHARDS:
        gf.sibling(i, j)

    def from_zed(k):
        return (g - k + 4) % 4

    for k in (1, 2, 3):
        o = from_zed(k)
        landed(F.at[pl.ds(SLAB + o * ROWS, ROWS)], zs.at[k - 1], zr.at[k - 1])

    for load in loads[3:]:
        load.wait()
    for r in range(2):
        rows = pl.ds(r * BLOCK, BLOCK)
        agg = jnp.zeros((BLOCK, D), F32)
        for k in range(K):
            b = cols[r, k]
            device = b // 2
            group, domain = device // N_DOM, device % N_DOM
            at = jnp.where(group == g, domain * 2 + b % 2, SLAB // BLOCK + group * 2 + b % 2)
            agg = agg + dot(adj[rows, k * BLOCK:(k + 1) * BLOCK], F[pl.ds(at * BLOCK, BLOCK), :])
        high = agg.astype(BF)
        rest = agg - high.astype(F32)
        low = rest.astype(BF)
        lowest = (rest - low.astype(F32)).astype(BF)
        AGG[pl.ds(c * ROWS + r * BLOCK, BLOCK), :] = high
        pre = (
            dot(F[pl.ds(d * ROWS + r * BLOCK, BLOCK), :], self_w[...])
            + (dot(high, nbr_w[...]) + (dot(low, nbr_w[...]) + dot(lowest, nbr_w[...])))
            + bias[...]
        )
        hidden = jnp.maximum(pre, 0.0)
        HID[rows, :] = hidden
        emb[rows, :] = hidden.astype(BF)
        Q[g, rows, :] = (hidden * rms_scale(hidden)).astype(BF)
        gt.to(5 + 2 * r)

    for k in (1, 3):
        send(Q.at[g], Q.at[g], zs.at[k + 5], zr.at[k + 5], zed(k))
    agg_own = AGG.at[pl.ds(c * ROWS, ROWS)]
    send(agg_own, agg_own, ms.at[0], mr.at[0], sib)
    emb_out = pltpu.make_async_copy(emb, emb_h, ls.at[8])
    emb_out.start()

    for k in (1, 2, 3):
        o = from_zed(k)
        landed(POS.at[o], zs.at[k + 2], zr.at[k + 2])
    lanes = lax.broadcasted_iota(jnp.int32, (ROWS, 128), 1).astype(F32)
    for o in range(N_GRP):
        PCOL[o] = column(POS[o, 0:1, :]) - lanes
    TACC[...] = jnp.zeros_like(TACC)
    PACC[...] = jnp.zeros_like(PACC)
    sib_rows = pl.ds((1 - c) * ROWS, ROWS)
    landed(AGG.at[sib_rows], ms.at[0], mr.at[0])
    pair = F[pl.ds((d // 2) * 2 * ROWS, 2 * ROWS), :]
    LT[...] = jnp.transpose(jnp.where(c == 0, pair, AGG[...]))
    drain(feature_sends)

    def doms_of(u, v):
        return [dom_at(i, j, c if v == 0 else 1 - c) for i, j in SHARDS[4 * u:4 * u + 4]]

    def offsets(dom):
        return [(g * SLAB + dom * ROWS + m * 128).astype(F32) for m in range(ROWS // 128)]

    def texts(u):
        doms = doms_of(u, 0) + doms_of(u, 1)
        ats = [at for dom in doms for at in offsets(dom)]
        return jnp.concatenate([T[pl.ds(dom * ROWS, ROWS), :] for dom in doms], axis=0), ats

    def exponentials(o, u):
        part, ats = texts(u)
        logits = dot_nt(Q[o], part)
        for r in range(0, ROWS, STRIP):
            rows = slice(r, r + STRIP)
            tot, picked, where = TACC[o, rows, :], PACC[o, rows, :], PCOL[o, rows, :]
            for m, at in enumerate(ats):
                tile = logits[rows, m * 128:(m + 1) * 128]
                e = jnp.exp2(tile * (SCALE * LOG2E))
                tot = tot + e
                picked = picked + jnp.where(where == at, tile, 0.0)
                lane = (m % 8) * 128
                base = (u * 2 + m // 8) * WIDE + o * ROWS + r
                FE[pl.ds(base, STRIP), lane:lane + 128] = e.astype(BF)
            TACC[o, rows, :] = tot
            PACC[o, rows, :] = picked

    def arrive(u):
        gt.to(UNITS[u])
        for i, j in SHARDS[4 * u:4 * u + 4]:
            gt.sibling(i, j)

    def queries(k):
        o = (g + k) % 4
        landed(Q.at[o], zs.at[9 - k], zr.at[9 - k])

    arrive(0)
    exponentials(g, 0)
    gt.to(11)
    arrive(1)
    send(Q.at[g], Q.at[g], zs.at[7], zr.at[7], zed(2))
    exponentials(g, 1)
    gt.to(17)
    for k, last in ((1, 19), (3, 23)):
        queries(k)
        for u in (0, 1):
            exponentials((g + k) % 4, u)
            gt.to(last + 2 * u if k == 1 else min(24, last + u))
    gt.to(24)
    arrive(2)
    for k in (0, 1, 3):
        exponentials((g + k) % 4, 2)
    queries(2)
    for u in range(3):
        exponentials((g + 2) % 4, u)
        gt.to((27, 29, 29)[u])
    arrive(3)
    for o in range(N_GRP):
        exponentials(o, 3)
        TP_S[o, 0:8, :] = lane_sums(TACC[o])
        TP_S[o, 8:16, :] = lane_sums(PACC[o])
        for k in (1, 2, 3):
            n = 8 + 4 * k + o - 3
            send(TP_S.at[o], TP_R.at[k - 1, o], zs.at[n], zr.at[n], zed(k))

    def totals(o):
        rows = TP_S[o]
        for k in (1, 2, 3):
            n = 8 + 4 * k + o - 3
            landed(TP_R.at[k - 1, o], zs.at[n], zr.at[n])
            rows = rows + TP_R[k - 1, o]
        return rows

    index = lax.broadcasted_iota(jnp.int32, (ROWS, 128), 0) % 64
    factor = 1.0 + (2 * index + 1).astype(F32) * (1.0 / 128)

    for o in range(N_GRP):
        rows = totals(o)
        RT[o] = factor / column(rows[0:1, :])
        TACC[o, 0:16, :] = rows[:, 0:128]
        TACC[o, 16:32, :] = rows[:, 128:256]

    def weigh(o, half):
        acc = jnp.zeros((HALF, H), F32)
        for u in range(4):
            part, ats = texts(u)
            strips = []
            for r in range(half * HALF, (half + 1) * HALF, STRIP):
                rows = slice(r, r + STRIP)
                inverse, where, unit = RT[o, rows, :], PCOL[o, rows, :], factor[rows, :]
                tiles = []
                for m, at in enumerate(ats):
                    lane = (m % 8) * 128
                    base = (u * 2 + m // 8) * WIDE + o * ROWS + r
                    e = FE[pl.ds(base, STRIP), lane:lane + 128]
                    w = e.astype(F32) * inverse
                    tiles.append((w - jnp.where(where == at, unit, 0.0)).astype(BF))
                strips.append(jnp.concatenate(tiles, axis=1))
            acc = acc + dot(jnp.concatenate(strips, axis=0), part)
        return acc

    for j in range(3):
        o = j + jnp.where(j < g, 0, 1)
        k = (o - g + 4) % 4
        for half in range(2):
            at = pl.ds(half * HALF, HALF)
            W_S[j, at, :] = weigh(o, half).astype(BF)
            send(
                W_S.at[j, at], W_R.at[k - 1, at],
                zs.at[21 + 2 * j + half], zr.at[19 + 2 * k + half], (o, d),
            )
    for half in range(2):
        W_O[pl.ds(half * HALF, HALF), :] = weigh(g, half)

    for k in (1, 2, 3):
        for half in range(2):
            n = 19 + 2 * k + half
            landed(W_R.at[k - 1, pl.ds(half * HALF, HALF)], zs.at[n], zr.at[n])

    unit = W_O[...]
    for k in range(3):
        unit = unit + W_R[k].astype(F32)
    unit = unit * (SCALE / factor[:, 0:1])
    lane_parts = jnp.concatenate([TACC[g, 0:16, :], TACC[g, 16:32, :]], axis=1)
    loss = jnp.sum(
        jnp.log(lane_parts[0:1, :]) - SCALE * lane_parts[8:9, :], axis=1, keepdims=True
    )
    hidden = HID[...]
    scale_rows = rms_scale(hidden)
    normed = hidden * scale_rows
    back = scale_rows * (unit - normed * jnp.mean(unit * normed, axis=1, keepdims=True))
    grad_pre = jnp.where(hidden > 0, back, 0.0)
    G[pl.ds(c * ROWS, ROWS), :] = grad_pre.astype(BF)
    g_own = G.at[pl.ds(c * ROWS, ROWS)]
    send(g_own, g_own, ms.at[1], mr.at[1], sib)

    bias_sum = jnp.sum(grad_pre, axis=0, keepdims=True)
    parts = [bias_sum[:, m * 128:(m + 1) * 128] for m in range(4)]
    parts.append(jnp.broadcast_to(loss, (1, 128)))
    parts.append(jnp.zeros((3, 128), F32))
    extra = split(jnp.concatenate(parts, axis=0))

    landed(G.at[sib_rows], ms.at[1], mr.at[1])

    for k in (1, 3, 2, 0):
        m = (pi + k) % 4
        columns = pl.ds(pl.multiple_of(m * 128, 128), 128)
        SA[m, 0:D, :] = dot(LT[...], G[:, columns]).astype(BF)
        SA[m, D:D + 16, :] = extra
        if k:
            send(SA.at[m], RA.at[k - 1], gs.at[k - 1], gr.at[k - 1], prim(k))
    total = SA[pi].astype(F32)
    for k in (1, 3, 2):
        landed(RA.at[k - 1], gs.at[k - 1], gr.at[k - 1])
        total = total + RA[k - 1].astype(F32)
    extra = split(join(total[D:D + 16, :]))

    for m in range(16):
        SB[m, 0:48, :] = total[m * 48:(m + 1) * 48, :].astype(BF)
        SB[m, 48:64, :] = extra
    me = si * 4 + g
    for n, (j, k) in enumerate(across):
        m = ((si + j) % 4) * 4 + (g + k) % 4
        send(SB.at[m], RB.at[n], gs.at[3 + n], gr.at[3 + n], wall(j, k))
    total = SB[me].astype(F32)
    for n in range(15):
        landed(RB.at[n], gs.at[3 + n], gr.at[3 + n])
        total = total + RB[n].astype(F32)

    EX[c] = split(join(total[48:64, :]))
    send(EX.at[c], EX.at[c], ms.at[2], mr.at[2], sib)

    def piece(j, k):
        return GR.at[c, pl.ds(pi * 768 + ((si + j + 4) % 4) * 192 + ((g + k + 4) % 4) * 48, 48)]

    GR[c, pl.ds(pi * 768 + si * 192 + g * 48, 48), :] = total[0:48, :].astype(BF)
    for n, (j, k) in enumerate(across):
        send(piece(0, 0), piece(0, 0), gs.at[18 + n], gr.at[18 + n], wall(j, k))
    for n, (j, k) in enumerate(across):
        landed(piece(-j, -k), gs.at[18 + n], gr.at[18 + n])

    def block(k, cc):
        index = x * (1 - cc) + y * cc
        return ((index + k + 4) % 4) * 768

    def both(k, cc):
        return GR.at[cc, pl.ds(block(k, cc), 768)]

    outs = []

    def write(k, cc):
        at = pl.ds(block(k, cc), 768)
        cp = pltpu.make_async_copy(GR.at[cc, at], grads_h.at[cc, at], ls.at[9 + len(outs)])
        cp.start()
        outs.append(cp)

    for k in (1, 3, 2):
        send(both(0, c), both(0, c), gs.at[32 + k], gr.at[32 + k], prim(k))
    send(both(0, c), both(0, c), ms.at[3], mr.at[3], sib)
    write(0, c)
    landed(EX.at[1 - c], ms.at[2], mr.at[2])
    XO[...] = join(EX[0].astype(F32)) + join(EX[1].astype(F32))
    extra_out = pltpu.make_async_copy(XO, extra_h, ls.at[17])
    extra_out.start()
    for k in (1, 3, 2):
        landed(both(-k, c), gs.at[32 + k], gr.at[32 + k])
        send(both(-k, c), both(-k, c), ms.at[3 + k], mr.at[3 + k], sib)
        write(-k, c)
    for k in (0, 1, 3, 2):
        landed(both(-k, 1 - c), ms.at[3 + k], mr.at[3 + k])
        write(-k, 1 - c)
    for cp in outs:
        cp.wait()
    emb_out.wait()
    extra_out.wait()
    drain(pending)


def finish(emb_in, grads, extra, emb, loss, grad_self, grad_nbr, grad_bias):
    emb[...] = emb_in[...]
    loss[...] = extra[4:5, 0:1] * (1.0 / NODES)
    for m in range(4):
        at = slice(m * 128, (m + 1) * 128)
        grad_self[:, at] = grads[0, m * D:(m + 1) * D, :].astype(F32)
        grad_nbr[:, at] = grads[1, m * D:(m + 1) * D, :].astype(F32)
        grad_bias[:, at] = extra[m:m + 1, :]


def shards(features, text_embed, adjacency, block_cols, positive, self_weight, nbr_weight, hidden_bias):
    vmem = pl.BlockSpec(memory_space=pltpu.VMEM)
    hbm = pl.BlockSpec(memory_space=pl.ANY)
    dma = pltpu.SemaphoreType.DMA
    emb, grads, extra = pl.pallas_call(
        kernel,
        name="step",
        out_shape=(
            jax.ShapeDtypeStruct((ROWS, H), BF),
            jax.ShapeDtypeStruct((2, 4 * D, 128), BF),
            jax.ShapeDtypeStruct((8, 128), F32),
        ),
        in_specs=[hbm] * 8,
        out_specs=(hbm,) * 3,
        scratch_shapes=[
            pltpu.VMEM((SLAB + N_GRP * ROWS, WIDE), BF),
            pltpu.VMEM((SLAB, H), BF),
            pltpu.VMEM((N_GRP, ROWS, H), BF),
            pltpu.VMEM((N_GRP, 8, ROWS), F32),
            pltpu.VMEM((N_GRP, ROWS, 128), F32),
            pltpu.VMEM((2 * ROWS, D), BF),
            pltpu.VMEM((ROWS, H), F32),
            pltpu.VMEM((2 * ROWS, H), BF),
            pltpu.VMEM((D, 2 * ROWS), BF),
            pltpu.VMEM((N_GRP, ROWS, 128), F32),
            pltpu.VMEM((N_GRP, ROWS, 128), F32),
            pltpu.VMEM((N_GRP, ROWS, 128), F32),
            pltpu.VMEM((3, ROWS, H), BF),
            pltpu.VMEM((3, ROWS, H), BF),
            pltpu.VMEM((ROWS, H), F32),
            pltpu.VMEM((N_GRP, 16, ROWS), F32),
            pltpu.VMEM((3, N_GRP, 16, ROWS), F32),
            pltpu.VMEM((4, D + 16, 128), BF),
            pltpu.VMEM((3, D + 16, 128), BF),
            pltpu.VMEM((16, 64, 128), BF),
            pltpu.VMEM((15, 64, 128), BF),
            pltpu.VMEM((2, 16, 128), BF),
            pltpu.VMEM((2, 4 * D, 128), BF),
            pltpu.VMEM((8, 128), F32),
            pltpu.VMEM((ROWS, H), BF),
            pltpu.VMEM((ROWS, K * BLOCK), BF),
            pltpu.SMEM((2, K), jnp.int32),
            pltpu.VMEM((1, ROWS), jnp.int32),
            pltpu.VMEM((D, H), BF),
            pltpu.VMEM((D, H), BF),
            pltpu.VMEM((1, H), F32),
            pltpu.VMEM((ROWS, H), BF),
            dma((GATHER_SEMS,)), dma((GATHER_SEMS,)),
            dma((GATHER_SEMS,)), dma((GATHER_SEMS,)),
            dma((30,)), dma((30,)),
            dma((7,)), dma((7,)),
            dma((36,)), dma((36,)),
            dma((18,)),
        ],
        compiler_params=pltpu.CompilerParams(
            collective_id=0, has_side_effects=True, vmem_limit_bytes=56 * 2**20
        ),
        cost_estimate=pl.CostEstimate(
            flops=20 * 10**9, bytes_accessed=8 * 2**20, transcendentals=8 * 2**20
        ),
    )(
        features, text_embed, adjacency, block_cols, positive.reshape(1, ROWS), self_weight,
        nbr_weight, hidden_bias.reshape(1, H),
    )
    emb, loss, grad_self, grad_nbr, grad_bias = pl.pallas_call(
        finish,
        name="finish",
        out_shape=(
            jax.ShapeDtypeStruct((ROWS, H), BF),
            jax.ShapeDtypeStruct((1, 1), F32),
            jax.ShapeDtypeStruct((D, H), F32),
            jax.ShapeDtypeStruct((D, H), F32),
            jax.ShapeDtypeStruct((1, H), F32),
        ),
        in_specs=[vmem] * 3,
        out_specs=(vmem,) * 5,
    )(emb, grads, extra)
    return emb, loss.reshape(()), grad_self, grad_nbr, grad_bias.reshape(H)


def solution(mesh):
    rows = P(("grp", "dom"), None)
    return jax.shard_map(
        shards,
        mesh=mesh,
        in_specs=(rows, rows, rows, rows, P(("grp", "dom")), P(), P(), P()),
        out_specs=(rows, P(), P(), P(), P()),
        check_vma=False,
    )
```

time: 138 us -> 136 us (0.986)
  Pallas kernels: 138 us -> 135 us
    pallas_call x1, Pallas kernels: 134 us -> 131 us  [shards(): pl.pallas_call(kernel, name='step', out_shape=(jax.ShapeDtypeStruct((ROWS...]
where the time goes in v3:
time: 136 us; the launch traced here: 135 us
  Pallas kernels  135 us (99%)
    pallas_call x1, Pallas kernels, shards(): pl.pallas_call(kernel, name='step', out_shape=(jax.ShapeDtypeStruct((ROWS...  131 us
    pallas_call x1, Pallas kernels, shards(): pl.pallas_call(finish, name='finish', out_shape=(jax.ShapeDtypeStruct((RO...  3.38 us

profile of v3, /device:TPU:1, one launch (start us, length us, event | category | flops | bytes accessed | tf_op | source)
XLA Modules:
  0.0 135.2 jit_solution(17700380074708781352)
XLA Ops:
  0.6 131.2 %step.1 = (bf16[256,512]{1,0:T(8,128)(2,1)}, bf16[2,3072,128]{2,1,0:T(8,128)(2,1)}, f32[8,128]{1,0:T(8,128)}) custom-call(bf16[256,768]{1,0:T(8,128)(2,1)} %feat_h.1, bf16[256,512]{1,0:T(8,128)(2,1)} %text_h.1, bf16[256,1024]{1,0:T(8,128)(2,1)} %adj_h.1, s32[2,8]{1,0:T(2,128)} %cols_h.1, s32[1,256]{1,0:T(1,128)} %bitcast.6, bf16[768,512]{1,0:T(8,128)(2,1)} %self_h.1, ...), custom_call_target="tpu_custom_call" | custom-call | flops 20000000000 | bytes 8388608 | tf_op jit(solution)/shard_map/step/pallas_call | solution.py:522
  131.8 3.4 %finish.1 = (bf16[256,512]{1,0:T(8,128)(2,1)}, f32[1,1]{1,0:T(1,128)}, f32[768,512]{1,0:T(8,128)}, f32[768,512]{1,0:T(8,128)}, f32[1,512]{1,0:T(1,128)}) custom-call(bf16[256,512]{1,0:T(8,128)(2,1)} %get-tuple-element.13.emb_in, bf16[2,3072,128]{2,1,0:T(8,128)(2,1)} %get-tuple-element.14.grads, f32[8,128]{1,0:T(8,128)} %get-tuple-element.15.extra), custom_call_target="tpu_custom_call" | custom-call | tf_op jit(solution)/shard_map/finish/pallas_call | solution.py:582

commit v4 on v3

--- a/solution.py
+++ b/solution.py
@@ -57,10 +57,7 @@
 
 
 def lane_sums(a):
-    return lax.dot_general(
-        jnp.ones((8, 128), F32), a, (((1,), (1,)), ((), ())),
-        precision=lax.Precision.HIGHEST, preferred_element_type=F32,
-    )
+    return jnp.sum(jnp.transpose(a), axis=0, keepdims=True)
 
 
 def split(v):
@@ -346,35 +343,30 @@
     arrive(3)
     for o in range(N_GRP):
         exponentials(o, 3)
-        TP_S[o, 0:8, :] = lane_sums(TACC[o])
-        TP_S[o, 8:16, :] = lane_sums(PACC[o])
-        for k in (1, 2, 3):
-            n = 8 + 4 * k + o - 3
-            send(TP_S.at[o], TP_R.at[k - 1, o], zs.at[n], zr.at[n], zed(k))
-
-    def totals(o):
-        rows = TP_S[o]
-        for k in (1, 2, 3):
-            n = 8 + 4 * k + o - 3
-            landed(TP_R.at[k - 1, o], zs.at[n], zr.at[n])
-            rows = rows + TP_R[k - 1, o]
-        return rows
+    for o in range(N_GRP):
+        TP_S[o] = jnp.concatenate(
+            [lane_sums(TACC[o]), lane_sums(PACC[o]), jnp.zeros((6, ROWS), F32)], axis=0
+        )
+    for k in (2, 1, 3):
+        send(TP_S, TP_R.at[k - 1], zs.at[8 + k], zr.at[8 + k], zed(k))
 
     index = lax.broadcasted_iota(jnp.int32, (ROWS, 128), 0) % 64
     factor = 1.0 + (2 * index + 1).astype(F32) * (1.0 / 128)
 
+    def totals(o):
+        return TP_S[o] + TP_R[0, o] + TP_R[1, o] + TP_R[2, o]
+
+    for k in (1, 3, 2):
+        landed(TP_R.at[k - 1], zs.at[8 + k], zr.at[8 + k])
     for o in range(N_GRP):
-        rows = totals(o)
-        RT[o] = factor / column(rows[0:1, :])
-        TACC[o, 0:16, :] = rows[:, 0:128]
-        TACC[o, 16:32, :] = rows[:, 128:256]
-
-    def weigh(o, half):
-        acc = jnp.zeros((HALF, H), F32)
+        RT[o] = factor / column(totals(o)[0:1, :])
+
+    def weigh(o):
+        acc = jnp.zeros((ROWS, H), F32)
         for u in range(4):
             part, ats = texts(u)
             strips = []
-            for r in range(half * HALF, (half + 1) * HALF, STRIP):
+            for r in range(0, ROWS, STRIP):
                 rows = slice(r, r + STRIP)
                 inverse, where, unit = RT[o, rows, :], PCOL[o, rows, :], factor[rows, :]
                 tiles = []
@@ -391,29 +383,19 @@
     for j in range(3):
         o = j + jnp.where(j < g, 0, 1)
         k = (o - g + 4) % 4
-        for half in range(2):
-            at = pl.ds(half * HALF, HALF)
-            W_S[j, at, :] = weigh(o, half).astype(BF)
-            send(
-                W_S.at[j, at], W_R.at[k - 1, at],
-                zs.at[21 + 2 * j + half], zr.at[19 + 2 * k + half], (o, d),
-            )
-    for half in range(2):
-        W_O[pl.ds(half * HALF, HALF), :] = weigh(g, half)
+        W_S[j] = weigh(o).astype(BF)
+        send(W_S.at[j], W_R.at[k - 1], zs.at[12 + j], zr.at[11 + k], (o, d))
+    W_O[...] = weigh(g)
 
     for k in (1, 2, 3):
-        for half in range(2):
-            n = 19 + 2 * k + half
-            landed(W_R.at[k - 1, pl.ds(half * HALF, HALF)], zs.at[n], zr.at[n])
+        landed(W_R.at[k - 1], zs.at[11 + k], zr.at[11 + k])
 
     unit = W_O[...]
     for k in range(3):
         unit = unit + W_R[k].astype(F32)
     unit = unit * (SCALE / factor[:, 0:1])
-    lane_parts = jnp.concatenate([TACC[g, 0:16, :], TACC[g, 16:32, :]], axis=1)
-    loss = jnp.sum(
-        jnp.log(lane_parts[0:1, :]) - SCALE * lane_parts[8:9, :], axis=1, keepdims=True
-    )
+    sums = totals(g)
+    loss = jnp.sum(jnp.log(sums[0:1, :]) - SCALE * sums[1:2, :], axis=1, keepdims=True)
     hidden = HID[...]
     scale_rows = rms_scale(hidden)
     normed = hidden * scale_rows
@@ -545,8 +527,8 @@
             pltpu.VMEM((3, ROWS, H), BF),
             pltpu.VMEM((3, ROWS, H), BF),
             pltpu.VMEM((ROWS, H), F32),
-            pltpu.VMEM((N_GRP, 16, ROWS), F32),
-            pltpu.VMEM((3, N_GRP, 16, ROWS), F32),
+            pltpu.VMEM((N_GRP, 8, ROWS), F32),
+            pltpu.VMEM((3, N_GRP, 8, ROWS), F32),
             pltpu.VMEM((4, D + 16, 128), BF),
             pltpu.VMEM((3, D + 16, 128), BF),
             pltpu.VMEM((16, 64, 128), BF),
@@ -564,7 +546,7 @@
             pltpu.VMEM((ROWS, H), BF),
             dma((GATHER_SEMS,)), dma((GATHER_SEMS,)),
             dma((GATHER_SEMS,)), dma((GATHER_SEMS,)),
-            dma((30,)), dma((30,)),
+            dma((15,)), dma((15,)),
             dma((7,)), dma((7,)),
             dma((36,)), dma((36,)),
             dma((18,)),

time: 136 us -> 134 us (0.985)
  Pallas kernels: 135 us -> 132 us
    pallas_call x1, Pallas kernels: 131 us -> 129 us  [shards(): pl.pallas_call(kernel, name='step', out_shape=(jax.ShapeDtypeStruct((ROWS...]
where the time goes in v4:
time: 134 us; the launch traced here: 133 us
  Pallas kernels  132 us (99%)
    pallas_call x1, Pallas kernels, shards(): pl.pallas_call(kernel, name='step', out_shape=(jax.ShapeDtypeStruct((ROWS...  129 us
    pallas_call x1, Pallas kernels, shards(): pl.pallas_call(finish, name='finish', out_shape=(jax.ShapeDtypeStruct((RO...  3.38 us

profile of v4, /device:TPU:1, one launch (start us, length us, event | category | flops | bytes accessed | tf_op | source)
XLA Modules:
  0.0 133.1 jit_solution(7473194426093508214)
XLA Ops:
  0.6 129.1 %step.1 = (bf16[256,512]{1,0:T(8,128)(2,1)}, bf16[2,3072,128]{2,1,0:T(8,128)(2,1)}, f32[8,128]{1,0:T(8,128)}) custom-call(bf16[256,768]{1,0:T(8,128)(2,1)} %feat_h.1, bf16[256,512]{1,0:T(8,128)(2,1)} %text_h.1, bf16[256,1024]{1,0:T(8,128)(2,1)} %adj_h.1, s32[2,8]{1,0:T(2,128)} %cols_h.1, s32[1,256]{1,0:T(1,128)} %bitcast.6, bf16[768,512]{1,0:T(8,128)(2,1)} %self_h.1, ...), custom_call_target="tpu_custom_call" | custom-call | flops 20000000000 | bytes 8388608 | tf_op jit(solution)/shard_map/step/pallas_call | solution.py:504
  129.7 3.4 %finish.1 = (bf16[256,512]{1,0:T(8,128)(2,1)}, f32[1,1]{1,0:T(1,128)}, f32[768,512]{1,0:T(8,128)}, f32[768,512]{1,0:T(8,128)}, f32[1,512]{1,0:T(1,128)}) custom-call(bf16[256,512]{1,0:T(8,128)(2,1)} %get-tuple-element.13.emb_in, bf16[2,3072,128]{2,1,0:T(8,128)(2,1)} %get-tuple-element.14.grads, f32[8,128]{1,0:T(8,128)} %get-tuple-element.15.extra), custom_call_target="tpu_custom_call" | custom-call | tf_op jit(solution)/shard_map/finish/pallas_call | solution.py:564

commit v5 on v4

--- a/solution.py
+++ b/solution.py
@@ -492,13 +492,12 @@
     loss[...] = extra[4:5, 0:1] * (1.0 / NODES)
     for m in range(4):
         at = slice(m * 128, (m + 1) * 128)
-        grad_self[:, at] = grads[0, m * D:(m + 1) * D, :].astype(F32)
-        grad_nbr[:, at] = grads[1, m * D:(m + 1) * D, :].astype(F32)
+        grad_self[:, at] = grads[0, m].astype(F32)
+        grad_nbr[:, at] = grads[1, m].astype(F32)
         grad_bias[:, at] = extra[m:m + 1, :]
 
 
 def shards(features, text_embed, adjacency, block_cols, positive, self_weight, nbr_weight, hidden_bias):
-    vmem = pl.BlockSpec(memory_space=pltpu.VMEM)
     hbm = pl.BlockSpec(memory_space=pl.ANY)
     dma = pltpu.SemaphoreType.DMA
     emb, grads, extra = pl.pallas_call(
@@ -571,9 +570,20 @@
             jax.ShapeDtypeStruct((D, H), F32),
             jax.ShapeDtypeStruct((1, H), F32),
         ),
-        in_specs=[vmem] * 3,
-        out_specs=(vmem,) * 5,
-    )(emb, grads, extra)
+        grid=(4,),
+        in_specs=[
+            pl.BlockSpec((ROWS // 4, H), lambda i: (i, 0)),
+            pl.BlockSpec((2, 4, D // 4, 128), lambda i: (0, 0, i, 0)),
+            pl.BlockSpec((8, 128), lambda i: (0, 0)),
+        ],
+        out_specs=(
+            pl.BlockSpec((ROWS // 4, H), lambda i: (i, 0)),
+            pl.BlockSpec((1, 1), lambda i: (0, 0)),
+            pl.BlockSpec((D // 4, H), lambda i: (i, 0)),
+            pl.BlockSpec((D // 4, H), lambda i: (i, 0)),
+            pl.BlockSpec((1, H), lambda i: (0, 0)),
+        ),
+    )(emb, grads.reshape(2, 4, D, 128), extra)
     return emb, loss.reshape(()), grad_self, grad_nbr, grad_bias.reshape(H)
 
 

time: 134 us -> 135 us (level)
  no operation moved by 1% of the time
where the time goes in v5:
time: 135 us; the launch traced here: 134 us
  Pallas kernels  133 us (99%)
    pallas_call x1, Pallas kernels, shards(): pl.pallas_call(kernel, name='step', out_shape=(jax.ShapeDtypeStruct((ROWS...  129 us
    pallas_call x1, Pallas kernels, shards(): pl.pallas_call(finish, name='finish', out_shape=(jax.ShapeDtypeStruct((RO...  4.08 us

profile of v5, /device:TPU:1, one launch (start us, length us, event | category | flops | bytes accessed | tf_op | source)
XLA Modules:
  0.0 133.8 jit_solution(316259540056569516)
XLA Ops:
  0.6 129.1 %step.1 = (bf16[256,512]{1,0:T(8,128)(2,1)}, bf16[2,3072,128]{2,1,0:T(8,128)(2,1)}, f32[8,128]{1,0:T(8,128)}) custom-call(bf16[256,768]{1,0:T(8,128)(2,1)} %feat_h.1, bf16[256,512]{1,0:T(8,128)(2,1)} %text_h.1, bf16[256,1024]{1,0:T(8,128)(2,1)} %adj_h.1, s32[2,8]{1,0:T(2,128)} %cols_h.1, s32[1,256]{1,0:T(1,128)} %bitcast.8, bf16[768,512]{1,0:T(8,128)(2,1)} %self_h.1, ...), custom_call_target="tpu_custom_call" | custom-call | flops 20000000000 | bytes 8388608 | tf_op jit(solution)/shard_map/step/pallas_call | solution.py:503
  129.7 4.1 %finish.1 = (bf16[256,512]{1,0:T(8,128)(2,1)}, f32[1,1]{1,0:T(1,128)}, f32[768,512]{1,0:T(8,128)}, f32[768,512]{1,0:T(8,128)}, f32[1,512]{1,0:T(1,128)}) custom-call(bf16[256,512]{1,0:T(8,128)(2,1)} %get-tuple-element.13.emb_in, bf16[2,4,768,128]{3,2,1,0:T(8,128)(2,1)} %bitcast.5, f32[8,128]{1,0:T(8,128)} %get-tuple-element.15.extra), custom_call_target="tpu_custom_call" | custom-call | tf_op jit(solution)/shard_map/finish/pallas_call | solution.py:563
